TPU v7x, 128 devices: a whole 4x4x4 slice. The times are simulated.
128 devices in a mesh: by: 8 (over y, core), bx: 16 (over z, x).
Axes of the slice: x: 4, y: 4, z: 4, core: 2. Of those that a mesh axis runs over, the one named last changes fastest.
Arguments:
- fields: float32 [3, 8, 2048, 4096], P(None, None, 'by', 'bx'), may hold values from -6 to 6
- level_count: int32 [2048, 4096], P('by', 'bx'), may hold values from 0 to 8, as said below
- thickness: float32 [8], replicated, may hold values from 0.05 to 0.3
- old_pressure: float32 [2048, 4096], P('by', 'bx'), may hold values from -6 to 6
Outputs:
- pressure: float32 [2048, 4096], P('by', 'bx')
- residual: float32 [2048, 4096], P('by', 'bx')
Inputs may be any that keep to these rules, and one draw needn't show every extreme that they name: `level_count`: land comes in aligned squares of 8 x 8 cells, except that the cell at row 1, column 0 is always ocean with all 8 levels.
All inputs are finite; a program needn't handle non-finite values.
Results may differ from a plain program's by a relative error of at most 0.00024.
Values sent between devices are 32-bit elements; how exact they have to be, the bound alone decides.
A program may use at most 128 MiB of HBM per device.

v0:
```python
import jax
import jax.numpy as jnp
from jax import lax
from jax.sharding import Mesh
from jax.sharding import PartitionSpec as P

ITERS = 4
BY_BX = ("by_0", "by_1", "bx_0", "bx_1")
BY = ("by_0", "by_1")
BX = ("bx_0", "bx_1")


VISCOSITY = 0.05
IMPLICIT = 0.05


def padded(array, sides, width):
    for axis, dim in sides:
        size, length = (lax.axis_size(axis), array.shape[dim])
        up = [(i, (i + 1) % size) for i in range(size)]
        down = [(j, i) for i, j in up]
        last = lax.slice_in_dim(array, length - width, length, axis=dim)
        initial = lax.slice_in_dim(array, 0, width, axis=dim)
        before = lax.ppermute(last, axis, up)
        after = lax.ppermute(initial, axis, down)
        array = jnp.concatenate([before, array, after], axis=dim)
    return array


def over_axes(array, axes):
    for axis in axes:
        array = lax.psum(array, axis)
    return array


def laplace(field):
    return (
        field[..., 1:-1, 2:]
        + field[..., 1:-1, :-2]
        + field[..., 2:, 1:-1]
        + field[..., :-2, 1:-1]
        - 4.0 * field[..., 1:-1, 1:-1]
    )


def level_divergence(extended):
    zonal = extended[0]
    meridional = extended[1]
    baroclinic = extended[2]
    tend_zonal = -VISCOSITY * laplace(laplace(zonal)) - 0.5 * (
        baroclinic[..., 2:-2, 3:-1] - baroclinic[..., 2:-2, 1:-3]
    )
    tend_merid = -VISCOSITY * laplace(laplace(meridional)) - 0.5 * (
        baroclinic[..., 3:-1, 2:-2] - baroclinic[..., 1:-3, 2:-2]
    )
    return 0.5 * (tend_zonal[..., 1:-1, 2:] - tend_zonal[..., 1:-1, :-2]) + 0.5 * (
        tend_merid[..., 2:, 1:-1] - tend_merid[..., :-2, 1:-1]
    )


def corner_min(extended_depth):
    return jnp.minimum(
        jnp.minimum(extended_depth[:-1, :-1], extended_depth[:-1, 1:]),
        jnp.minimum(extended_depth[1:, :-1], extended_depth[1:, 1:]),
    )


def operate(extended, corner):
    west_south = extended[:-1, :-1]
    east_south = extended[:-1, 1:]
    west_north = extended[1:, :-1]
    east_north = extended[1:, 1:]
    east_slope = 0.5 * (east_south + east_north - west_south - west_north)
    north_slope = 0.5 * (west_north + east_north - west_south - east_south)
    plus_flux = 0.5 * corner * (east_slope + north_slope)
    minus_flux = 0.5 * corner * (east_slope - north_slope)
    return (
        IMPLICIT * extended[1:-1, 1:-1]
        + plus_flux[:-1, :-1]
        - plus_flux[1:, 1:]
        + minus_flux[1:, :-1]
        - minus_flux[:-1, 1:]
    )


def tile_extend(field):
    return padded(field, ((BY, 0), (BX, 1)), 1)


def paired_dots(residual, precond, image_field):
    return (
        over_axes(jnp.sum(residual * precond), BY_BX),
        over_axes(jnp.sum(precond * image_field), BY_BX),
    )


def solve(right_side, column_depth, first_guess, extend):
    corner = corner_min(extend(column_depth))
    diagonal = IMPLICIT + 0.5 * (
        corner[1:, 1:] + corner[1:, :-1] + corner[:-1, 1:] + corner[:-1, :-1]
    )
    pressure = first_guess
    residual = right_side - operate(extend(pressure), corner)
    precond = residual / diagonal
    image_field = operate(extend(precond), corner)
    norm_now, curvature = paired_dots(residual, precond, image_field)
    step_length = norm_now / curvature
    direction = precond
    image_dir = image_field
    for iteration in range(ITERS):
        pressure = pressure + step_length * direction
        residual = residual - step_length * image_dir
        if iteration + 1 < ITERS:
            precond = residual / diagonal
            image_field = operate(extend(precond), corner)
            norm_next, curvature = paired_dots(residual, precond, image_field)
            ratio_next = norm_next / norm_now
            step_length = norm_next / (curvature - ratio_next * norm_next / step_length)
            direction = precond + ratio_next * direction
            image_dir = image_field + ratio_next * image_dir
            norm_now = norm_next
    return (pressure, residual)


def shards(fields, level_count, thickness, old_pressure):
    levels = jnp.arange(thickness.shape[0], dtype=jnp.int32)[:, None, None]
    wet_mask = (levels < level_count[None]).astype(jnp.float32)
    weights = thickness[:, None, None] * wet_mask
    column_depth = jnp.sum(weights, axis=0)
    extended = padded(fields, ((BY, 2), (BX, 3)), 3)
    forcing_sum = jnp.sum(weights * level_divergence(extended), axis=0)
    ocean_mask = (level_count > 0).astype(jnp.float32)
    right_side = ocean_mask * (forcing_sum + IMPLICIT * old_pressure)
    first_guess = ocean_mask * old_pressure
    pressure, residual = solve(right_side, column_depth, first_guess, tile_extend)
    return (pressure, residual)


def solution(mesh):
    torus = Mesh(mesh.devices.reshape(4, 2, 4, 4), ("by_0", "by_1", "bx_0", "bx_1"))
    in_specs = (P(None, None, BY, BX), P(BY, BX), P(), P(BY, BX))
    out_specs = (P(BY, BX), P(BY, BX))
    return jax.shard_map(
        shards, mesh=torus, in_specs=in_specs, out_specs=out_specs, check_vma=False
    )
```

profile of v0, /device:TPU:1, one launch (start us, length us, event | category | flops | bytes accessed | tf_op | source)
XLA Modules:
  0.0 291.2 jit_solution(12813563485470110456)
XLA Ops:
  1.7 2.7 collective-permute-start
  6.8 6.8 %copy.16 = f32[3,8,256,256]{2,1,3,0:T(8,128)} copy(f32[3,8,256,256]{3,2,1,0:T(8,128)} %param.4) | data formatting | bytes 12582912 | tf_op args[0]
  13.6 2.3 copy.15
  15.9 2.2 copy.17
  20.7 5.0 %collective-permute-start.3 = (f32[3,8,262,3]{2,1,3,0:T(8,128)S(1)}, f32[3,8,262,3]{2,1,3,0:T(8,128)S(1)}, u32[]{:S(2)}, u32[]{:S(2)}) collective-permute-start(f32[3,8,262,3]{2,1,3,0:T(8,128)S(1)} %get-tuple-element.78), channel_id=1, source_target_pairs={{1,0},{2,1},{3,2},{4,3},{5,4},{6,5},{7,6},{8,7},{9,8},{10,9},{11,1... | collective-permute-start | bytes 226376 | tf_op jit(solution)/shard_map/ppermute | solution.py:25
  26.4 2.0 collective-permute-start.8
  28.5 6.3 %pad_maximum_fusion = f32[3,8,262,262]{2,1,3,0:T(8,128)} fusion(f32[3,8,262,3]{2,1,3,0:T(8,128)S(1)} %collective-permute-done.3, f32[3,8,3,256]{2,1,3,0:T(8,128)S(1)} %copy-done.1, f32[3,8,256,256]{2,1,3,0:T(8,128)S(1)} %bitcast.7, f32[3,8,3,256]{2,1,3,0:T(8,128)S(1)} %copy-done, f32[3,8,262,3]{2,1,3,0:T(8,128)S(1)} %collective-permute-done.2), kind=kLoop, calls=%fused_computation | loop fusion | flops 6589824 | bytes 13179648 | tf_op jit(solution)/shard_map/concatenate | solution.py:26
  34.9 6.1 %slice_bitcast_fusion.2 = (f32[8,262,262]{1,0,2:T(8,128)S(1)}, f32[8,262,262]{1,0,2:T(8,128)S(1)}, f32[8,262,262]{1,0,2:T(8,128)}) fusion(f32[3,8,262,262]{2,1,3,0:T(8,128)} %pad_maximum_fusion), kind=kLoop, calls=%fused_computation.3 | loop fusion | bytes 13179648 | tf_op jit(solution)/shard_map/squeeze | solution.py:47
  41.0 7.0 %fusion = (f32[8,260,260]{1,0,2:T(8,128)S(1)}, f32[8,260,260]{1,0,2:T(8,128)S(1)}) fusion(f32[8,262,262]{1,0,2:T(8,128)S(1)} %get-tuple-element.80, f32[8,262,262]{1,0,2:T(8,128)S(1)} %get-tuple-element.79), kind=kLoop, calls=%fused_computation.5 | loop fusion | flops 5408000 | bytes 25958400 | tf_op jit(solution)/shard_map/sub | solution.py:38
  48.0 17.4 %fusion.7 = (f32[8,258,258]{1,0,2:T(8,128)}, f32[8,258,258]{1,0,2:T(8,128)}) fusion(f32[8,262,262]{1,0,2:T(8,128)} %get-tuple-element.81, f32[8,260,260]{1,0,2:T(8,128)S(1)} %get-tuple-element.123, f32[8,260,260]{1,0,2:T(8,128)S(1)} %get-tuple-element.122), kind=kLoop, calls=%fused_computation.25 | loop fusion | flops 9585216 | bytes 34080768 | tf_op jit(solution)/shard_map/sub | solution.py:50
  65.4 6.4 %fusion.10 = (f32[256,256]{0,1:T(8,128)S(1)}, f32[256,256]{0,1:T(8,128)S(1)}) fusion(f32[8,258,258]{1,0,2:T(8,128)} %get-tuple-element.85, f32[8,258,258]{1,0,2:T(8,128)} %get-tuple-element.84, f32[8]{0:T(128)S(1)} %copy-done.5, s32[256,256]{0,1:T(8,128)} %copy-done.4), kind=kLoop, calls=%fused_computation.34 | loop fusion | flops 4587520 | bytes 9175072 | tf_op jit(solution)/shard_map/reduce_sum | solution.py:131
  71.8 2.1 collective-permute-start.4
  75.6 4.2 %collective-permute-start.10 = (f32[258,1]{0,1:T(1,128)S(1)}, f32[258,1]{0,1:T(1,128)S(1)}, u32[]{:S(2)}, u32[]{:S(2)}) collective-permute-start(f32[258,1]{0,1:T(1,128)S(1)} %get-tuple-element.109), channel_id=1, source_target_pairs={{1,0},{2,1},{3,2},{4,3},{5,4},{6,5},{7,6},{8,7},{9,8},{10,9},{11,1... | collective-permute-start | bytes 3104 | tf_op jit(solution)/shard_map/ppermute | solution.py:25
  79.9 4.8 %collective-permute-start.7 = (f32[258,1]{0,1:T(1,128)S(1)}, f32[258,1]{0,1:T(1,128)S(1)}, u32[]{:S(2)}, u32[]{:S(2)}) collective-permute-start(f32[258,1]{0,1:T(1,128)S(1)} %get-tuple-element.105), channel_id=1, source_target_pairs={{1,0},{2,1},{3,2},{4,3},{5,4},{6,5},{7,6},{8,7},{9,8},{10,9},{11,1... | collective-permute-start | bytes 3104 | tf_op jit(solution)/shard_map/ppermute | solution.py:25
  88.9 3.2 %collective-permute-start.12 = (f32[1,256]{0,1:T(8,128)S(1)}, f32[1,256]{0,1:T(8,128)S(1)}, u32[]{:S(2)}, u32[]{:S(2)}) collective-permute-start(f32[1,256]{0,1:T(8,128)S(1)} %get-tuple-element.116), channel_id=1, source_target_pairs={{0,16},{16,32},{32,48},{48,64},{64,80},{80,96},{96,112},{112,0},{1... | collective-permute-start | bytes 3080 | tf_op jit(solution)/shard_map/ppermute | solution.py:24
  94.0 2.4 collective-permute-done.13
  96.5 3.8 %collective-permute-start.14 = (f32[258,1]{0,1:T(1,128)S(1)}, f32[258,1]{0,1:T(1,128)S(1)}, u32[]{:S(2)}, u32[]{:S(2)}) collective-permute-start(f32[258,1]{0,1:T(1,128)S(1)} %get-tuple-element.101), channel_id=1, source_target_pairs={{1,0},{2,1},{3,2},{4,3},{5,4},{6,5},{7,6},{8,7},{9,8},{10,9},{11,1... | collective-permute-start | bytes 3104 | tf_op jit(solution)/shard_map/ppermute | solution.py:25
  101.0 5.0 %collective-permute-done.15 = f32[258,1]{0,1:T(1,128)S(1)} collective-permute-done((f32[258,1]{0,1:T(1,128)S(1)}, f32[258,1]{0,1:T(1,128)S(1)}, u32[]{:S(2)}, u32[]{:S(2)}) %collective-permute-start.15) | collective-permute-done | bytes 1064 | tf_op jit(solution)/shard_map/ppermute | solution.py:24
  107.6 11.7 %all-reduce.11 = (f32[]{:T(128)}, f32[]{:T(128)}) all-reduce(f32[]{:T(128)} %get-tuple-element.13, f32[]{:T(128)} %get-tuple-element.12), channel_id=1, replica_groups=mesh['by_0'=4,'by_1'=2,'bx_0'=4,'bx_1'=4] {'by_0'}, use_global_device_ids=true, to_apply=%region_3.0 | all-reduce | flops 2 | bytes 16 | tf_op jit(solution)/shard_map/psum | solution.py:32
  119.3 3.1 %all-reduce.15 = (f32[]{:T(128)}, f32[]{:T(128)}) all-reduce(f32[]{:T(128)} %get-tuple-element.36, f32[]{:T(128)} %get-tuple-element.37), channel_id=1, replica_groups=mesh['by_0'=4,'by_1'=2,'bx_0'=4,'bx_1'=4] {'by_1'}, use_global_device_ids=true, to_apply=%region_4.0 | all-reduce | flops 2 | bytes 16 | tf_op jit(solution)/shard_map/psum | solution.py:32
  122.4 6.7 %all-reduce.7 = (f32[]{:T(128)}, f32[]{:T(128)}) all-reduce(f32[]{:T(128)} %get-tuple-element.44, f32[]{:T(128)} %get-tuple-element.45), channel_id=1, replica_groups=mesh['by_0'=4,'by_1'=2,'bx_0'=4,'bx_1'=4] {'bx_0'}, use_global_device_ids=true, to_apply=%region_5.0 | all-reduce | flops 2 | bytes 16 | tf_op jit(solution)/shard_map/psum | solution.py:32
  129.1 6.6 %all-reduce.3 = (f32[]{:T(128)}, f32[]{:T(128)}) all-reduce(f32[]{:T(128)} %get-tuple-element.28, f32[]{:T(128)} %get-tuple-element.29), channel_id=1, replica_groups=mesh['by_0'=4,'by_1'=2,'bx_0'=4,'bx_1'=4] {'bx_1'}, use_global_device_ids=true, to_apply=%region_6.0 | all-reduce | flops 2 | bytes 16 | tf_op jit(solution)/shard_map/psum | solution.py:32
  137.2 5.9 %collective-permute-start.16 = (f32[1,256]{0,1:T(8,128)S(1)}, f32[1,256]{0,1:T(8,128)S(1)}, u32[]{:S(2)}, u32[]{:S(2)}) collective-permute-start(f32[1,256]{0,1:T(8,128)S(1)} %get-tuple-element.114), channel_id=1, source_target_pairs={{0,16},{16,32},{32,48},{48,64},{64,80},{80,96},{96,112},{112,0},{1... | collective-permute-start | bytes 3080 | tf_op jit(solution)/shard_map/ppermute | solution.py:24
  143.1 1.9 collective-permute-done.16
  145.1 2.4 collective-permute-done.17
  147.6 2.6 collective-permute-start.18
  151.0 5.0 %collective-permute-done.19 = f32[258,1]{0,1:T(1,128)S(1)} collective-permute-done((f32[258,1]{0,1:T(1,128)S(1)}, f32[258,1]{0,1:T(1,128)S(1)}, u32[]{:S(2)}, u32[]{:S(2)}) %collective-permute-start.19) | collective-permute-done | bytes 1064 | tf_op jit(solution)/shard_map/ppermute | solution.py:24
  157.6 9.0 %all-reduce.10 = (f32[]{:T(128)}, f32[]{:T(128)}) all-reduce(f32[]{:T(128)} %get-tuple-element.11, f32[]{:T(128)} %get-tuple-element.10), channel_id=1, replica_groups=mesh['by_0'=4,'by_1'=2,'bx_0'=4,'bx_1'=4] {'by_0'}, use_global_device_ids=true, to_apply=%region_13.0 | all-reduce | flops 2 | bytes 16 | tf_op jit(solution)/shard_map/psum | solution.py:32
  166.5 4.0 %all-reduce.14 = (f32[]{:T(128)}, f32[]{:T(128)}) all-reduce(f32[]{:T(128)} %get-tuple-element.34, f32[]{:T(128)} %get-tuple-element.35), channel_id=1, replica_groups=mesh['by_0'=4,'by_1'=2,'bx_0'=4,'bx_1'=4] {'by_1'}, use_global_device_ids=true, to_apply=%region_14.0 | all-reduce | flops 2 | bytes 16 | tf_op jit(solution)/shard_map/psum | solution.py:32
  170.6 6.8 %all-reduce.6 = (f32[]{:T(128)}, f32[]{:T(128)}) all-reduce(f32[]{:T(128)} %get-tuple-element.42, f32[]{:T(128)} %get-tuple-element.43), channel_id=1, replica_groups=mesh['by_0'=4,'by_1'=2,'bx_0'=4,'bx_1'=4] {'bx_0'}, use_global_device_ids=true, to_apply=%region_15.0 | all-reduce | flops 2 | bytes 16 | tf_op jit(solution)/shard_map/psum | solution.py:32
  177.3 6.6 %all-reduce.2 = (f32[]{:T(128)}, f32[]{:T(128)}) all-reduce(f32[]{:T(128)} %get-tuple-element.26, f32[]{:T(128)} %get-tuple-element.27), channel_id=1, replica_groups=mesh['by_0'=4,'by_1'=2,'bx_0'=4,'bx_1'=4] {'bx_1'}, use_global_device_ids=true, to_apply=%region_16.0 | all-reduce | flops 2 | bytes 16 | tf_op jit(solution)/shard_map/psum | solution.py:32
  188.6 5.1 %collective-permute-start.20 = (f32[1,256]{0,1:T(8,128)S(1)}, f32[1,256]{0,1:T(8,128)S(1)}, u32[]{:S(2)}, u32[]{:S(2)}) collective-permute-start(f32[1,256]{0,1:T(8,128)S(1)} %get-tuple-element.112), channel_id=1, source_target_pairs={{0,16},{16,32},{32,48},{48,64},{64,80},{80,96},{96,112},{112,0},{1... | collective-permute-start | bytes 3080 | tf_op jit(solution)/shard_map/ppermute | solution.py:24
  193.7 1.9 collective-permute-done.20
  195.7 2.4 collective-permute-done.21
  198.2 2.6 collective-permute-start.22
  201.6 5.0 %collective-permute-done.23 = f32[258,1]{0,1:T(1,128)S(1)} collective-permute-done((f32[258,1]{0,1:T(1,128)S(1)}, f32[258,1]{0,1:T(1,128)S(1)}, u32[]{:S(2)}, u32[]{:S(2)}) %collective-permute-start.23) | collective-permute-done | bytes 1064 | tf_op jit(solution)/shard_map/ppermute | solution.py:24
  208.2 9.8 %all-reduce.9 = (f32[]{:T(128)}, f32[]{:T(128)}) all-reduce(f32[]{:T(128)} %get-tuple-element.9, f32[]{:T(128)} %get-tuple-element.8), channel_id=1, replica_groups=mesh['by_0'=4,'by_1'=2,'bx_0'=4,'bx_1'=4] {'by_0'}, use_global_device_ids=true, to_apply=%region_23.0 | all-reduce | flops 2 | bytes 16 | tf_op jit(solution)/shard_map/psum | solution.py:32
  218.0 3.1 %all-reduce.13 = (f32[]{:T(128)}, f32[]{:T(128)}) all-reduce(f32[]{:T(128)} %get-tuple-element.32, f32[]{:T(128)} %get-tuple-element.33), channel_id=1, replica_groups=mesh['by_0'=4,'by_1'=2,'bx_0'=4,'bx_1'=4] {'by_1'}, use_global_device_ids=true, to_apply=%region_24.0 | all-reduce | flops 2 | bytes 16 | tf_op jit(solution)/shard_map/psum | solution.py:32
  221.1 6.7 %all-reduce.5 = (f32[]{:T(128)}, f32[]{:T(128)}) all-reduce(f32[]{:T(128)} %get-tuple-element.40, f32[]{:T(128)} %get-tuple-element.41), channel_id=1, replica_groups=mesh['by_0'=4,'by_1'=2,'bx_0'=4,'bx_1'=4] {'bx_0'}, use_global_device_ids=true, to_apply=%region_25.0 | all-reduce | flops 2 | bytes 16 | tf_op jit(solution)/shard_map/psum | solution.py:32
  227.8 6.9 %all-reduce.1 = (f32[]{:T(128)}, f32[]{:T(128)}) all-reduce(f32[]{:T(128)} %get-tuple-element.24, f32[]{:T(128)} %get-tuple-element.25), channel_id=1, replica_groups=mesh['by_0'=4,'by_1'=2,'bx_0'=4,'bx_1'=4] {'bx_1'}, use_global_device_ids=true, to_apply=%region_26.0 | all-reduce | flops 2 | bytes 16 | tf_op jit(solution)/shard_map/psum | solution.py:32
  238.8 5.6 %collective-permute-start.24 = (f32[1,256]{0,1:T(8,128)S(1)}, f32[1,256]{0,1:T(8,128)S(1)}, u32[]{:S(2)}, u32[]{:S(2)}) collective-permute-start(f32[1,256]{0,1:T(8,128)S(1)} %get-tuple-element.110), channel_id=1, source_target_pairs={{0,16},{16,32},{32,48},{48,64},{64,80},{80,96},{96,112},{112,0},{1... | collective-permute-start | bytes 3080 | tf_op jit(solution)/shard_map/ppermute | solution.py:24
  246.4 2.4 collective-permute-done.25
  248.9 2.6 collective-permute-start.26
  252.3 5.0 %collective-permute-done.27 = f32[258,1]{0,1:T(1,128)S(1)} collective-permute-done((f32[258,1]{0,1:T(1,128)S(1)}, f32[258,1]{0,1:T(1,128)S(1)}, u32[]{:S(2)}, u32[]{:S(2)}) %collective-permute-start.27) | collective-permute-done | bytes 1064 | tf_op jit(solution)/shard_map/ppermute | solution.py:24
  259.0 8.9 %all-reduce.8 = (f32[]{:T(128)}, f32[]{:T(128)}) all-reduce(f32[]{:T(128)} %get-tuple-element.7, f32[]{:T(128)} %get-tuple-element.6), channel_id=1, replica_groups=mesh['by_0'=4,'by_1'=2,'bx_0'=4,'bx_1'=4] {'by_0'}, use_global_device_ids=true, to_apply=%region_33.0 | all-reduce | flops 2 | bytes 16 | tf_op jit(solution)/shard_map/psum | solution.py:32
  267.9 4.1 %all-reduce.12 = (f32[]{:T(128)}, f32[]{:T(128)}) all-reduce(f32[]{:T(128)} %get-tuple-element.30, f32[]{:T(128)} %get-tuple-element.31), channel_id=1, replica_groups=mesh['by_0'=4,'by_1'=2,'bx_0'=4,'bx_1'=4] {'by_1'}, use_global_device_ids=true, to_apply=%region_34.0 | all-reduce | flops 2 | bytes 16 | tf_op jit(solution)/shard_map/psum | solution.py:32
  272.0 6.7 %all-reduce.4 = (f32[]{:T(128)}, f32[]{:T(128)}) all-reduce(f32[]{:T(128)} %get-tuple-element.38, f32[]{:T(128)} %get-tuple-element.39), channel_id=1, replica_groups=mesh['by_0'=4,'by_1'=2,'bx_0'=4,'bx_1'=4] {'bx_0'}, use_global_device_ids=true, to_apply=%region_35.0 | all-reduce | flops 2 | bytes 16 | tf_op jit(solution)/shard_map/psum | solution.py:32
  278.7 6.7 %all-reduce = (f32[]{:T(128)}, f32[]{:T(128)}) all-reduce(f32[]{:T(128)} %get-tuple-element.22, f32[]{:T(128)} %get-tuple-element.23), channel_id=1, replica_groups=mesh['by_0'=4,'by_1'=2,'bx_0'=4,'bx_1'=4] {'bx_1'}, use_global_device_ids=true, to_apply=%region_36.0 | all-reduce | flops 2 | bytes 16 | tf_op jit(solution)/shard_map/psum | solution.py:32
  (96 shorter events, 28.5 us)
Async XLA Ops:
  1.7 11.9 %collective-permute-start = (f32[3,8,3,256]{3,1,2,0:T(8,128)S(1)}, f32[3,8,3,256]{3,1,2,0:T(8,128)S(1)}, u32[]{:S(2)}, u32[]{:S(2)}) collective-permute-start(f32[3,8,3,256]{3,1,2,0:T(8,128)S(1)} %copy.21), channel_id=1, source_target_pairs={{0,16},{16,32},{32,48},{48,64},{64,80},{80,96},{96,112},{112,0},{1... | collective-permute-start | bytes 221192 | tf_op jit(solution)/shard_map/ppermute | solution.py:24
  4.4 11.5 %collective-permute-start.1 = (f32[3,8,3,256]{3,1,2,0:T(8,128)S(1)}, f32[3,8,3,256]{3,1,2,0:T(8,128)S(1)}, u32[]{:S(2)}, u32[]{:S(2)}) collective-permute-start(f32[3,8,3,256]{3,1,2,0:T(8,128)S(1)} %copy.22), channel_id=1, source_target_pairs={{16,0},{32,16},{48,32},{64,48},{80,64},{96,80},{112,96},{0,112},{1... | collective-permute-start | bytes 221192 | tf_op jit(solution)/shard_map/ppermute | solution.py:25
  5.5 8.1 %copy-start.4 = (s32[256,256]{0,1:T(8,128)}, s32[256,256]{0,1:T(8,128)S(1)}, u32[]{:S(2)}) copy-start(s32[256,256]{0,1:T(8,128)S(1)} %copy.10) | copy-start | bytes 786436
  6.7 6.9 %copy-start.2 = (f32[256,256]{0,1:T(8,128)}, f32[256,256]{0,1:T(8,128)S(1)}, u32[]{:S(2)}) copy-start(f32[256,256]{0,1:T(8,128)S(1)} %copy.11) | copy-start | bytes 786436
  15.9 12.6 %slice-start = ((s8[6291456]{0:T(1024)(128)(4,1)}), s8[2097152]{0:T(1024)(128)(4,1)S(1)}, s32[]{:S(2)}) async-start(s8[6291456]{0:T(1024)(128)(4,1)} %bitcast.6), calls=%async_computation | async-start | bytes 4194304
  18.1 10.4 %slice-start.1 = ((s8[6291456]{0:T(1024)(128)(4,1)}), s8[4194304]{0:T(1024)(128)(4,1)S(1)}, s32[]{:S(2)}) async-start(s8[6291456]{0:T(1024)(128)(4,1)} %bitcast.6), calls=%async_computation.1 | async-start | bytes 8388608
  18.1 10.4 %copy-start = (f32[3,8,3,256]{2,1,3,0:T(8,128)S(1)}, f32[3,8,3,256]{2,1,3,0:T(8,128)}, u32[]{:S(2)}) copy-start(f32[3,8,3,256]{2,1,3,0:T(8,128)} %copy.15) | copy-start | bytes 221188
  18.1 10.4 %copy-start.1 = (f32[3,8,3,256]{2,1,3,0:T(8,128)S(1)}, f32[3,8,3,256]{2,1,3,0:T(8,128)}, u32[]{:S(2)}) copy-start(f32[3,8,3,256]{2,1,3,0:T(8,128)} %copy.17) | copy-start | bytes 221188
  19.4 9.1 %collective-permute-start.2 = (f32[3,8,262,3]{2,1,3,0:T(8,128)S(1)}, f32[3,8,262,3]{2,1,3,0:T(8,128)S(1)}, u32[]{:S(2)}, u32[]{:S(2)}) collective-permute-start(f32[3,8,262,3]{2,1,3,0:T(8,128)S(1)} %get-tuple-element.77), channel_id=1, source_target_pairs={{0,1},{1,2},{2,3},{3,4},{4,5},{5,6},{6,7},{7,8},{8,9},{9,10},{10,1... | collective-permute-start | bytes 226376 | tf_op jit(solution)/shard_map/ppermute | solution.py:24
  20.7 7.8 %collective-permute-start.3 = (f32[3,8,262,3]{2,1,3,0:T(8,128)S(1)}, f32[3,8,262,3]{2,1,3,0:T(8,128)S(1)}, u32[]{:S(2)}, u32[]{:S(2)}) collective-permute-start(f32[3,8,262,3]{2,1,3,0:T(8,128)S(1)} %get-tuple-element.78), channel_id=1, source_target_pairs={{1,0},{2,1},{3,2},{4,3},{5,4},{6,5},{7,6},{8,7},{9,8},{10,9},{11,1... | collective-permute-start | bytes 226376 | tf_op jit(solution)/shard_map/ppermute | solution.py:25
  26.4 48.4 %collective-permute-start.8 = (f32[1,256]{0,1:T(8,128)}, f32[1,256]{0,1:T(8,128)}, u32[]{:S(2)}, u32[]{:S(2)}) collective-permute-start(f32[1,256]{0,1:T(8,128)} %get-tuple-element.120), channel_id=1, source_target_pairs={{0,16},{16,32},{32,48},{48,64},{64,80},{80,96},{96,112},{112,0},{1... | collective-permute-start | bytes 3080 | tf_op jit(solution)/shard_map/ppermute | solution.py:24
  28.5 46.4 %collective-permute-start.9 = (f32[1,256]{0,1:T(8,128)}, f32[1,256]{0,1:T(8,128)}, u32[]{:S(2)}, u32[]{:S(2)}) collective-permute-start(f32[1,256]{0,1:T(8,128)} %get-tuple-element.121), channel_id=1, source_target_pairs={{16,0},{32,16},{48,32},{64,48},{80,64},{96,80},{112,96},{0,112},{1... | collective-permute-start | bytes 3080 | tf_op jit(solution)/shard_map/ppermute | solution.py:25
  48.0 17.4 %copy-start.5 = (f32[8]{0:T(128)S(1)}, f32[8]{0:T(128)}, u32[]{:S(2)}) copy-start(f32[8]{0:T(128)} %param.6) | copy-start | bytes 100
  71.8 8.0 %collective-permute-start.4 = (f32[1,256]{0,1:T(8,128)S(1)}, f32[1,256]{0,1:T(8,128)S(1)}, u32[]{:S(2)}, u32[]{:S(2)}) collective-permute-start(f32[1,256]{0,1:T(8,128)S(1)} %get-tuple-element.118), channel_id=1, source_target_pairs={{0,16},{16,32},{32,48},{48,64},{64,80},{80,96},{96,112},{112,0},{1... | collective-permute-start | bytes 3080 | tf_op jit(solution)/shard_map/ppermute | solution.py:24
  74.0 5.9 %collective-permute-start.5 = (f32[1,256]{0,1:T(8,128)S(1)}, f32[1,256]{0,1:T(8,128)S(1)}, u32[]{:S(2)}, u32[]{:S(2)}) collective-permute-start(f32[1,256]{0,1:T(8,128)S(1)} %get-tuple-element.119), channel_id=1, source_target_pairs={{16,0},{32,16},{48,32},{64,48},{80,64},{96,80},{112,96},{0,112},{1... | collective-permute-start | bytes 3080 | tf_op jit(solution)/shard_map/ppermute | solution.py:25
  75.6 9.2 %collective-permute-start.10 = (f32[258,1]{0,1:T(1,128)S(1)}, f32[258,1]{0,1:T(1,128)S(1)}, u32[]{:S(2)}, u32[]{:S(2)}) collective-permute-start(f32[258,1]{0,1:T(1,128)S(1)} %get-tuple-element.109), channel_id=1, source_target_pairs={{1,0},{2,1},{3,2},{4,3},{5,4},{6,5},{7,6},{8,7},{9,8},{10,9},{11,1... | collective-permute-start | bytes 3104 | tf_op jit(solution)/shard_map/ppermute | solution.py:25
  79.8 5.8 %collective-permute-start.11 = (f32[258,1]{0,1:T(1,128)S(1)}, f32[258,1]{0,1:T(1,128)S(1)}, u32[]{:S(2)}, u32[]{:S(2)}) collective-permute-start(f32[258,1]{0,1:T(1,128)S(1)} %get-tuple-element.108), channel_id=1, source_target_pairs={{0,1},{1,2},{2,3},{3,4},{4,5},{5,6},{6,7},{7,8},{8,9},{9,10},{10,1... | collective-permute-start | bytes 3104 | tf_op jit(solution)/shard_map/ppermute | solution.py:24
  79.9 7.1 %collective-permute-start.6 = (f32[258,1]{0,1:T(1,128)S(1)}, f32[258,1]{0,1:T(1,128)S(1)}, u32[]{:S(2)}, u32[]{:S(2)}) collective-permute-start(f32[258,1]{0,1:T(1,128)S(1)} %get-tuple-element.104), channel_id=1, source_target_pairs={{0,1},{1,2},{2,3},{3,4},{4,5},{5,6},{6,7},{7,8},{8,9},{9,10},{10,1... | collective-permute-start | bytes 3104 | tf_op jit(solution)/shard_map/ppermute | solution.py:24
  79.9 7.1 %collective-permute-start.7 = (f32[258,1]{0,1:T(1,128)S(1)}, f32[258,1]{0,1:T(1,128)S(1)}, u32[]{:S(2)}, u32[]{:S(2)}) collective-permute-start(f32[258,1]{0,1:T(1,128)S(1)} %get-tuple-element.105), channel_id=1, source_target_pairs={{1,0},{2,1},{3,2},{4,3},{5,4},{6,5},{7,6},{8,7},{9,8},{10,9},{11,1... | collective-permute-start | bytes 3104 | tf_op jit(solution)/shard_map/ppermute | solution.py:25
  87.4 1.0 copy-start.3
  88.9 5.1 %collective-permute-start.12 = (f32[1,256]{0,1:T(8,128)S(1)}, f32[1,256]{0,1:T(8,128)S(1)}, u32[]{:S(2)}, u32[]{:S(2)}) collective-permute-start(f32[1,256]{0,1:T(8,128)S(1)} %get-tuple-element.116), channel_id=1, source_target_pairs={{0,16},{16,32},{32,48},{48,64},{64,80},{80,96},{96,112},{112,0},{1... | collective-permute-start | bytes 3080 | tf_op jit(solution)/shard_map/ppermute | solution.py:24
  92.0 4.4 %collective-permute-start.13 = (f32[1,256]{0,1:T(8,128)S(1)}, f32[1,256]{0,1:T(8,128)S(1)}, u32[]{:S(2)}, u32[]{:S(2)}) collective-permute-start(f32[1,256]{0,1:T(8,128)S(1)} %get-tuple-element.117), channel_id=1, source_target_pairs={{16,0},{32,16},{48,32},{64,48},{80,64},{96,80},{112,96},{0,112},{1... | collective-permute-start | bytes 3080 | tf_op jit(solution)/shard_map/ppermute | solution.py:25
  96.5 4.5 %collective-permute-start.14 = (f32[258,1]{0,1:T(1,128)S(1)}, f32[258,1]{0,1:T(1,128)S(1)}, u32[]{:S(2)}, u32[]{:S(2)}) collective-permute-start(f32[258,1]{0,1:T(1,128)S(1)} %get-tuple-element.101), channel_id=1, source_target_pairs={{1,0},{2,1},{3,2},{4,3},{5,4},{6,5},{7,6},{8,7},{9,8},{10,9},{11,1... | collective-permute-start | bytes 3104 | tf_op jit(solution)/shard_map/ppermute | solution.py:25
  100.3 5.8 %collective-permute-start.15 = (f32[258,1]{0,1:T(1,128)S(1)}, f32[258,1]{0,1:T(1,128)S(1)}, u32[]{:S(2)}, u32[]{:S(2)}) collective-permute-start(f32[258,1]{0,1:T(1,128)S(1)} %get-tuple-element.100), channel_id=1, source_target_pairs={{0,1},{1,2},{2,3},{3,4},{4,5},{5,6},{6,7},{7,8},{8,9},{9,10},{10,1... | collective-permute-start | bytes 3104 | tf_op jit(solution)/shard_map/ppermute | solution.py:24
  137.2 7.9 %collective-permute-start.16 = (f32[1,256]{0,1:T(8,128)S(1)}, f32[1,256]{0,1:T(8,128)S(1)}, u32[]{:S(2)}, u32[]{:S(2)}) collective-permute-start(f32[1,256]{0,1:T(8,128)S(1)} %get-tuple-element.114), channel_id=1, source_target_pairs={{0,16},{16,32},{32,48},{48,64},{64,80},{80,96},{96,112},{112,0},{1... | collective-permute-start | bytes 3080 | tf_op jit(solution)/shard_map/ppermute | solution.py:24
  143.1 4.4 %collective-permute-start.17 = (f32[1,256]{0,1:T(8,128)S(1)}, f32[1,256]{0,1:T(8,128)S(1)}, u32[]{:S(2)}, u32[]{:S(2)}) collective-permute-start(f32[1,256]{0,1:T(8,128)S(1)} %get-tuple-element.115), channel_id=1, source_target_pairs={{16,0},{32,16},{48,32},{64,48},{80,64},{96,80},{112,96},{0,112},{1... | collective-permute-start | bytes 3080 | tf_op jit(solution)/shard_map/ppermute | solution.py:25
  147.6 3.4 %collective-permute-start.18 = (f32[258,1]{0,1:T(1,128)S(1)}, f32[258,1]{0,1:T(1,128)S(1)}, u32[]{:S(2)}, u32[]{:S(2)}) collective-permute-start(f32[258,1]{0,1:T(1,128)S(1)} %get-tuple-element.97), channel_id=1, source_target_pairs={{1,0},{2,1},{3,2},{4,3},{5,4},{6,5},{7,6},{8,7},{9,8},{10,9},{11,1... | collective-permute-start | bytes 3104 | tf_op jit(solution)/shard_map/ppermute | solution.py:25
  150.2 5.8 %collective-permute-start.19 = (f32[258,1]{0,1:T(1,128)S(1)}, f32[258,1]{0,1:T(1,128)S(1)}, u32[]{:S(2)}, u32[]{:S(2)}) collective-permute-start(f32[258,1]{0,1:T(1,128)S(1)} %get-tuple-element.96), channel_id=1, source_target_pairs={{0,1},{1,2},{2,3},{3,4},{4,5},{5,6},{6,7},{7,8},{8,9},{9,10},{10,1... | collective-permute-start | bytes 3104 | tf_op jit(solution)/shard_map/ppermute | solution.py:24
  188.6 7.1 %collective-permute-start.20 = (f32[1,256]{0,1:T(8,128)S(1)}, f32[1,256]{0,1:T(8,128)S(1)}, u32[]{:S(2)}, u32[]{:S(2)}) collective-permute-start(f32[1,256]{0,1:T(8,128)S(1)} %get-tuple-element.112), channel_id=1, source_target_pairs={{0,16},{16,32},{32,48},{48,64},{64,80},{80,96},{96,112},{112,0},{1... | collective-permute-start | bytes 3080 | tf_op jit(solution)/shard_map/ppermute | solution.py:24
  193.7 4.4 %collective-permute-start.21 = (f32[1,256]{0,1:T(8,128)S(1)}, f32[1,256]{0,1:T(8,128)S(1)}, u32[]{:S(2)}, u32[]{:S(2)}) collective-permute-start(f32[1,256]{0,1:T(8,128)S(1)} %get-tuple-element.113), channel_id=1, source_target_pairs={{16,0},{32,16},{48,32},{64,48},{80,64},{96,80},{112,96},{0,112},{1... | collective-permute-start | bytes 3080 | tf_op jit(solution)/shard_map/ppermute | solution.py:25
  198.2 3.4 %collective-permute-start.22 = (f32[258,1]{0,1:T(1,128)S(1)}, f32[258,1]{0,1:T(1,128)S(1)}, u32[]{:S(2)}, u32[]{:S(2)}) collective-permute-start(f32[258,1]{0,1:T(1,128)S(1)} %get-tuple-element.93), channel_id=1, source_target_pairs={{1,0},{2,1},{3,2},{4,3},{5,4},{6,5},{7,6},{8,7},{9,8},{10,9},{11,1... | collective-permute-start | bytes 3104 | tf_op jit(solution)/shard_map/ppermute | solution.py:25
  200.8 5.8 %collective-permute-start.23 = (f32[258,1]{0,1:T(1,128)S(1)}, f32[258,1]{0,1:T(1,128)S(1)}, u32[]{:S(2)}, u32[]{:S(2)}) collective-permute-start(f32[258,1]{0,1:T(1,128)S(1)} %get-tuple-element.92), channel_id=1, source_target_pairs={{0,1},{1,2},{2,3},{3,4},{4,5},{5,6},{6,7},{7,8},{8,9},{9,10},{10,1... | collective-permute-start | bytes 3104 | tf_op jit(solution)/shard_map/ppermute | solution.py:24
  238.8 7.6 %collective-permute-start.24 = (f32[1,256]{0,1:T(8,128)S(1)}, f32[1,256]{0,1:T(8,128)S(1)}, u32[]{:S(2)}, u32[]{:S(2)}) collective-permute-start(f32[1,256]{0,1:T(8,128)S(1)} %get-tuple-element.110), channel_id=1, source_target_pairs={{0,16},{16,32},{32,48},{48,64},{64,80},{80,96},{96,112},{112,0},{1... | collective-permute-start | bytes 3080 | tf_op jit(solution)/shard_map/ppermute | solution.py:24
  244.4 4.4 %collective-permute-start.25 = (f32[1,256]{0,1:T(8,128)S(1)}, f32[1,256]{0,1:T(8,128)S(1)}, u32[]{:S(2)}, u32[]{:S(2)}) collective-permute-start(f32[1,256]{0,1:T(8,128)S(1)} %get-tuple-element.111), channel_id=1, source_target_pairs={{16,0},{32,16},{48,32},{64,48},{80,64},{96,80},{112,96},{0,112},{1... | collective-permute-start | bytes 3080 | tf_op jit(solution)/shard_map/ppermute | solution.py:25
  248.9 3.4 %collective-permute-start.26 = (f32[258,1]{0,1:T(1,128)S(1)}, f32[258,1]{0,1:T(1,128)S(1)}, u32[]{:S(2)}, u32[]{:S(2)}) collective-permute-start(f32[258,1]{0,1:T(1,128)S(1)} %get-tuple-element.89), channel_id=1, source_target_pairs={{1,0},{2,1},{3,2},{4,3},{5,4},{6,5},{7,6},{8,7},{9,8},{10,9},{11,1... | collective-permute-start | bytes 3104 | tf_op jit(solution)/shard_map/ppermute | solution.py:25
  251.6 5.8 %collective-permute-start.27 = (f32[258,1]{0,1:T(1,128)S(1)}, f32[258,1]{0,1:T(1,128)S(1)}, u32[]{:S(2)}, u32[]{:S(2)}) collective-permute-start(f32[258,1]{0,1:T(1,128)S(1)} %get-tuple-element.88), channel_id=1, source_target_pairs={{0,1},{1,2},{2,3},{3,4},{4,5},{5,6},{6,7},{7,8},{8,9},{9,10},{10,1... | collective-permute-start | bytes 3104 | tf_op jit(solution)/shard_map/ppermute | solution.py:24
where the time goes:
time: 295 us; the launch traced here: 291 us
  blocking collectives  107 us (36%)
  starting transfers between devices  55.8 us (19%)
  other arithmetic  49.1 us (17%)
  waiting for transfers between devices  40.3 us (14%)
  local copies, waits for them, and re-layouts  24 us (8%)
  between operations  14.7 us (5%)
    psum x16, blocking collectives, over_axes(): array = lax.psum(array, axis)  107 us
    ppermute x14, starting transfers between devices, padded(): before = lax.ppermute(last, axis, up)  28 us
    ppermute x14, starting transfers between devices, padded(): after = lax.ppermute(initial, axis, down)  27.8 us
    ppermute x14, waiting for transfers between devices, padded(): before = lax.ppermute(last, axis, up)  27.6 us
    sub x1, other arithmetic, level_divergence(): -VISCOSITY * laplace(laplace(zonal))  17.4 us
    ppermute x14, waiting for transfers between devices, padded(): after = lax.ppermute(initial, axis, down)  12.7 us
    unnamed x23, local copies, waits for them, and re-layouts  11.1 us
    concatenate x12, other arithmetic, padded(): array = jnp.concatenate([before, array, after], axis=dim)  10.6 us
  transfers between devices with their start and end apart: 28, of which 17 were waited for; matrix products, arithmetic and copies ran while one was open for 20% of the time, Pallas kernels for 0%

commit v1 on v0

v1 whole, which is shorter than its diff:
```python
import functools

import jax
import jax.numpy as jnp
from jax import lax
from jax.experimental import pallas as pl
from jax.experimental.pallas import tpu as pltpu
from jax.sharding import PartitionSpec as P

VISCOSITY = 0.05
IMPLICIT = 0.05
ITERS = 4
MESH = pl.DeviceIdType.MESH

LANES = 128
SUB = 8
HALO = 8
PAD = 8


def lane_ids():
    return lax.broadcasted_iota(jnp.int32, (SUB, LANES), 1)


def roll(x, shift):
    return pltpu.roll(x, shift % LANES, axis=1)


def from_east(tiles, lane, by=1):
    rolled = [None if x is None else roll(x, -by) for x in tiles]
    out = []
    for n in range(len(tiles)):
        a, b = rolled[n], rolled[(n + 1) % len(tiles)]
        a = 0.0 if a is None else a
        b = 0.0 if b is None else b
        out.append(jnp.where(lane >= LANES - by, b, a))
    return out


def from_west(tiles, lane, by=1):
    rolled = [None if x is None else roll(x, by) for x in tiles]
    out = []
    for n in range(len(tiles)):
        a, b = rolled[n], rolled[n - 1]
        a = 0.0 if a is None else a
        b = 0.0 if b is None else b
        out.append(jnp.where(lane < by, b, a))
    return out


def scalars(nu):
    half = 0.5

    def times_b(s):
        return [s[1]] + [half * (s[n + 1] + s[n - 1]) for n in range(1, len(s) - 1)]

    def coef_b(c):
        out = [None] * (len(c) + 1)

        def put(n, x):
            out[n] = x if out[n] is None else out[n] + x

        for n, x in enumerate(c):
            if n == 0:
                put(1, x)
            else:
                put(n + 1, half * x)
                put(n - 1, half * x)
        zero = jnp.zeros_like(c[0])
        return [zero if x is None else x for x in out]

    def plus(a, b):
        n = max(len(a), len(b))
        return [
            a[m] + b[m] if m < len(a) and m < len(b) else (a[m] if m < len(a) else b[m])
            for m in range(n)
        ]

    one = jnp.ones_like(nu[0])
    s_z, s_d = list(nu), list(nu)
    c_z, c_d = [one], [one]
    c_p = []
    norm = nu[0]
    for it in range(ITERS):
        b = times_b(s_d)
        s_a = [s_d[n] - b[n] for n in range(len(b))]
        b = coef_b(c_d)
        c_a = plus(c_d, [-x for x in b])
        alpha = norm / (c_d[it] * s_a[it])
        c_p = plus(c_p, [alpha * x for x in c_d])
        c_z = plus(c_z, [-(alpha * x) for x in c_a])
        if it + 1 < ITERS:
            s_z = [s_z[n] - alpha * s_a[n] for n in range(len(s_a))]
            new = c_z[it + 1] * s_z[it + 1]
            beta = new / norm
            norm = new
            s_d = [s_z[n] + beta * s_d[n] for n in range(len(s_z))]
            c_d = plus(c_z, [beta * x for x in c_d])
    return c_p, c_z


def kernel(
    dims,
    th,
    fields,
    level_count,
    old_pressure,
    out_p,
    out_r,
    fb,
    lev,
    lp,
    pack,
    got1,
    got1d,
    fv,
    fr,
    ft,
    fold,
    got2y,
    got2x,
    got2d,
    c00,
    c0m,
    dm,
    dinv,
    q0,
    tk,
    mom,
    ar1,
    ar2,
    ores,
    load_sem,
    field_sem,
    send1,
    recv1,
    send2,
    recv2,
    sendr,
    recvr,
    sendc,
    recvc,
    out_sem,
):
    ny, nx, km, rows = dims
    ext = rows + 2 * HALO
    T = ext // SUB
    own = rows // SUB
    me_y, me_x = lax.axis_index("by"), lax.axis_index("bx")
    lane = lane_ids()
    sub = lax.broadcasted_iota(jnp.int32, (SUB, LANES), 0)
    zero = jnp.zeros((SUB, LANES), jnp.float32)

    loads = []
    for c in range(2):
        cols = pl.ds(c * LANES, LANES)
        loads.append(pltpu.make_async_copy(level_count.at[:, cols], lev.at[c], load_sem.at[c]))
        loads.append(
            pltpu.make_async_copy(
                old_pressure.at[:, cols], lp.at[1, c, pl.ds(PAD + HALO, rows)], load_sem.at[2 + c]
            )
        )
    for x in loads:
        x.start()

    def field_copy(k, c):
        return pltpu.make_async_copy(
            fields.at[:, k, :, pl.ds(c * LANES, LANES)],
            fb.at[:, k, c, pl.ds(PAD + HALO, rows)],
            field_sem.at[k, c],
        )

    for k in range(km):
        for c in range(2):
            field_copy(k, c).start()

    def peer(dy, dx):
        return (lax.rem(me_y + dy + ny, ny), lax.rem(me_x + dx + nx, nx))

    peers = [peer(dy, 0) for dy in range(1, ny)] + [peer(0, dx) for dx in range(1, nx)]
    peers += [peer(dy, dx) for dy in (1, -1) for dx in (1, -1)]
    barrier = pltpu.get_barrier_semaphore()
    for x in peers:
        pl.semaphore_signal(barrier, inc=1, device_id=x, device_id_type=MESH)

    def clear(k, carry):
        for f in range(3):
            for c in range(2):
                for r in (0, 8, rows + 16, rows + 24):
                    fb[f, k, c, pl.ds(r, SUB), :] = zero
        return carry

    lax.fori_loop(0, km, clear, 0)
    for n in range(2):
        for c in range(3):
            lp[n, c, pl.ds(0, SUB), :] = zero
            lp[n, c, pl.ds(ext + PAD, SUB), :] = zero

    def clear_sum(t, carry):
        for c in range(3):
            fv[t, c] = zero
            tk[0, t, c] = zero
        return carry

    lax.fori_loop(0, T, clear_sum, 0)

    for x in loads:
        x.wait()
    packed = [[zero] * 4, [zero] * 4]
    for r in range(own):
        at = pl.ds(PAD + HALO + r * SUB, SUB)
        group, pos = r % 8, r // 8
        mask = (lane >= 16 * group) & (lane < 16 * group + 16)
        for c in range(2):
            lp[0, c, at, :] = lev[c, pl.ds(r * SUB, SUB), :].astype(jnp.float32)
        east = jnp.where(lane >= 120, lp[0, 1, at, :], roll(lp[1, 1, at, :], -8))
        west = jnp.where(lane < 8, lp[0, 0, at, :], roll(lp[1, 0, at, :], 8))
        packed[0][pos] = jnp.where(mask, roll(east, 16 * group + 16), packed[0][pos])
        packed[1][pos] = jnp.where(mask, roll(west, 16 * group), packed[1][pos])
    for side in range(2):
        for pos in range(4):
            pack[side, pl.ds(pos * SUB, SUB), :] = packed[side][pos]
    pl.semaphore_wait(barrier, len(peers))

    def remote(src, dst, send, recv, n, target):
        return pltpu.make_async_remote_copy(
            src_ref=src,
            dst_ref=dst,
            send_sem=send.at[n],
            recv_sem=recv.at[n],
            device_id=target,
            device_id_type=MESH,
        )

    low, high = PAD + HALO, PAD + HALO + rows - SUB
    tiles01 = pl.ds(0, 2)
    first = [
        remote(lp.at[:, tiles01, pl.ds(high, SUB)], lp.at[:, tiles01, pl.ds(PAD, SUB)], send1, recv1, 0, peer(1, 0)),
        remote(lp.at[:, tiles01, pl.ds(low, SUB)], lp.at[:, tiles01, pl.ds(high + SUB, SUB)], send1, recv1, 1, peer(-1, 0)),
        remote(pack.at[0], got1.at[0], send1, recv1, 2, peer(0, 1)),
        remote(pack.at[1], got1.at[1], send1, recv1, 3, peer(0, -1)),
        remote(pack.at[0, pl.ds(24, SUB)], got1d.at[0], send1, recv1, 4, peer(1, 1)),
        remote(pack.at[1, pl.ds(24, SUB)], got1d.at[1], send1, recv1, 5, peer(1, -1)),
        remote(pack.at[0, pl.ds(0, SUB)], got1d.at[2], send1, recv1, 6, peer(-1, 1)),
        remote(pack.at[1, pl.ds(0, SUB)], got1d.at[3], send1, recv1, 7, peer(-1, -1)),
    ]
    for x in first:
        x.start()
    for x in first:
        x.wait_recv()

    def place(at, west_side, east_side, group):
        lev_w = roll(west_side, 112 - 16 * group)
        old_w = roll(west_side, 120 - 16 * group)
        lev_e = roll(east_side, -16 * group)
        old_e = roll(east_side, -16 * group - 8)
        lp[0, 2, at, :] = jnp.where(lane < 64, lev_e, lev_w)
        lp[1, 2, at, :] = jnp.where(lane < 64, old_e, old_w)

    for r in range(own):
        row = pl.ds((r // 8) * SUB, SUB)
        place(pl.ds(low + r * SUB, SUB), got1[0, row, :], got1[1, row, :], r % 8)
    place(pl.ds(PAD, SUB), got1d[0], got1d[1], 7)
    place(pl.ds(high + SUB, SUB), got1d[2], got1d[3], 0)

    def row_of(t):
        return pl.ds(t + PAD, SUB, stride=T)

    def level(k, carry):
        for c in range(2):
            field_copy(k, c).wait()
        weight = th[k] * (-0.5 * VISCOSITY)
        here = k.astype(jnp.float32)
        u, v, p, g, h = {}, {}, {}, {}, {}

        def load(f, t):
            return [fb[f, k, c, row_of(t), :] for c in range(2)]

        for step in range(-3, T + 3):
            v[step] = load(1, step)
            t = step - 1
            if -2 <= t:
                w = load(0, t) + [None]
                e, o = from_east(w, lane), from_west(w, lane)
                g[t] = [
                    (e[0] - o[0]) + (v[t + 1][0] - v[t - 1][0]),
                    (e[1] - o[1]) + (v[t + 1][1] - v[t - 1][1]),
                    e[2] - o[2],
                ]
                p[t] = load(2, t)
                v.pop(t - 1)
            t = step - 2
            if -1 <= t:
                e, o = from_east(g[t], lane), from_west(g[t], lane)
                h[t] = [
                    (e[c] + o[c]) + (g[t + 1][c] + g[t - 1][c]) - 4.0 * g[t][c] for c in range(3)
                ]
                g.pop(t - 1)
            t = step - 3
            if 0 <= t:
                e, o = from_east(h[t], lane), from_west(h[t], lane)
                ee, oo = from_east(p[t] + [None], lane, 2), from_west(p[t] + [None], lane, 2)
                for c in range(3):
                    bi = (e[c] + o[c]) + (h[t + 1][c] + h[t - 1][c]) - 4.0 * h[t][c]
                    pr = ee[c] + oo[c]
                    if c < 2:
                        pr = pr + (p[t + 2][c] + p[t - 2][c]) - 4.0 * p[t][c]
                    term = bi + (0.5 / VISCOSITY) * pr
                    wet = jnp.where(lp[0, c, row_of(t), :] > here, weight, 0.0)
                    fv[t, c] += wet * term
                h.pop(t - 1)
                p.pop(t - 2)
        return carry

    lax.fori_loop(0, km, level, 0)

    for t in range(T):
        for c in range(3):
            fr[c, pl.ds(t, SUB, stride=T), :] = fv[t, c]
    folded = [[zero] * 3, [zero] * 3]
    for r in range(T):
        at = pl.ds(r * SUB, SUB)
        group, pos = r % 12, r // 12
        mask = (lane >= 8 * group) & (lane < 8 * group + 8)
        east = roll(jnp.where(lane < 64, fr[2, at, :], fr[1, at, :]), 4 + 8 * group)
        west = roll(jnp.where(lane < 64, fr[0, at, :], fr[2, at, :]), 4 + 8 * group)
        folded[0][pos] = jnp.where(mask, east, folded[0][pos])
        folded[1][pos] = jnp.where(mask, west, folded[1][pos])
    for side in range(2):
        for pos in range(3):
            fold[side, pl.ds(pos * SUB, SUB), :] = folded[side][pos]
    second = [
        remote(fr.at[:, pl.ds(ext - 16, 16)], got2y.at[0], send2, recv2, 0, peer(1, 0)),
        remote(fr.at[:, pl.ds(0, 16)], got2y.at[1], send2, recv2, 1, peer(-1, 0)),
        remote(fold.at[0], got2x.at[0], send2, recv2, 2, peer(0, 1)),
        remote(fold.at[1], got2x.at[1], send2, recv2, 3, peer(0, -1)),
        remote(fold.at[0, pl.ds(16, SUB)], got2d.at[0], send2, recv2, 4, peer(1, 1)),
        remote(fold.at[1, pl.ds(16, SUB)], got2d.at[1], send2, recv2, 5, peer(1, -1)),
        remote(fold.at[0, pl.ds(0, SUB)], got2d.at[2], send2, recv2, 6, peer(-1, 1)),
        remote(fold.at[1, pl.ds(0, SUB)], got2d.at[3], send2, recv2, 7, peer(-1, -1)),
    ]
    for x in second:
        x.start()

    def depth_of(t):
        out = []
        for c in range(3):
            count = lp[0, c, row_of(t), :]
            total = jnp.where(count > 0.0, th[0], 0.0)
            for k in range(1, km):
                total = total + jnp.where(count > float(k), th[k], 0.0)
            out.append(total)
        return out

    def guess_of(t):
        return [jnp.where(lp[0, c, row_of(t), :] > 0.0, lp[1, c, row_of(t), :], 0.0) for c in range(3)]

    depth, mid, west, up, down = {-1: depth_of(-1)}, {}, {}, {}, {}
    for step in range(-1, T + 1):
        t = step
        if t < T:
            depth[t + 1] = depth_of(t + 1)
            low2 = [jnp.minimum(depth[t][c], depth[t + 1][c]) for c in range(3)]
            e = from_east(low2, lane)
            mid[t] = [0.5 * jnp.minimum(low2[c], e[c]) for c in range(3)]
            west[t] = from_west(mid[t], lane)
            depth.pop(t)
            for c in range(3):
                c00[t + 1, c] = mid[t][c]
                c0m[t + 1, c] = west[t][c]
        guess = guess_of(t)
        e, o = from_east(guess, lane), from_west(guess, lane)
        if t < T:
            down[t] = [mid[t][c] * e[c] + west[t][c] * o[c] for c in range(3)]
        if t >= 0:
            up[t] = [mid[t - 1][c] * e[c] + west[t - 1][c] * o[c] for c in range(3)]
        t = step - 1
        if t >= 0:
            guess = guess_of(t)
            for c in range(3):
                k_sum = (mid[t][c] + mid[t - 1][c]) + (west[t][c] + west[t - 1][c])
                diagonal = IMPLICIT + k_sum
                dinv[t, c] = 1.0 / diagonal
                q0[t, c] = (up[t + 1][c] + down[t - 1][c]) - k_sum * guess[c]
                if c < 2:
                    if t < HALO:
                        diagonal = jnp.where(sub == 0, 0.0, diagonal)
                    if t >= T - HALO:
                        diagonal = jnp.where(sub == SUB - 1, 0.0, diagonal)
                    dm[t, c] = diagonal
            mid.pop(t - 1), west.pop(t - 1), up.pop(t, None), down.pop(t - 1)

    for x in second:
        x.wait_recv()
    for r in range(T):
        at = pl.ds(r * SUB, SUB)
        group, pos = r % 12, pl.ds((r // 12) * SUB, SUB)
        shift = -(4 + 8 * group)
        east = roll(got2x[0, pos, :], shift)
        west_ = roll(got2x[1, pos, :], shift)
        total = [fr[c, at, :] for c in range(3)]
        if r < 2:
            total = [total[c] + got2y[0, c, at, :] for c in range(3)]
            east = east + roll(got2d[0], -(4 + 8 * (8 + r)))
            west_ = west_ + roll(got2d[1], -(4 + 8 * (8 + r)))
        if r >= T - 2:
            row = pl.ds((r - T + 2) * SUB, SUB)
            total = [total[c] + got2y[1, c, row, :] for c in range(3)]
            east = east + roll(got2d[2], -(4 + 8 * (r - T + 2)))
            west_ = west_ + roll(got2d[3], -(4 + 8 * (r - T + 2)))
        ft[0, at, :] = total[0] + jnp.where(lane < 4, east, 0.0)
        ft[1, at, :] = total[1] + jnp.where(lane >= 124, west_, 0.0)
        ft[2, at, :] = total[2] + jnp.where(lane < 4, west_, jnp.where(lane >= 124, east, 0.0))

    acc = [zero, zero]
    for t in range(T):
        for c in range(3):
            force = ft[c, pl.ds(t, SUB, stride=T), :]
            wet = lp[0, c, row_of(t), :] > 0.0
            z = (jnp.where(wet, force, 0.0) + q0[t, c]) * dinv[t, c]
            tk[1, t, c] = z
            if c < 2:
                acc[c] = acc[c] + (dm[t, c] * z) * z
    mom[0] = acc[0] + acc[1]

    def power(k, carry):
        factor = jnp.where(k == 0, 1.0, 2.0)

        def products(t):
            w = [tk[k + 1, t, c] for c in range(3)]
            e, o = from_east(w, lane), from_west(w, lane)
            dn = [c00[t + 1, c] * e[c] + c0m[t + 1, c] * o[c] for c in range(3)]
            up_ = [c00[t, c] * e[c] + c0m[t, c] * o[c] for c in range(3)]
            return w, dn, up_

        w_of, dn_of, up_of = {}, {}, {}
        w_of[T - 1], dn_of[T - 1], up_of[T - 1] = products(T - 1)
        dn_of[-1] = [pltpu.roll(x, 1, axis=0) for x in dn_of[T - 1]]
        w_of[0], dn_of[0], up_of[0] = products(0)
        up_of[T] = [pltpu.roll(x, SUB - 1, axis=0) for x in up_of[0]]
        odd, even = [zero, zero], [zero, zero]
        for t in range(T):
            if t + 1 < T - 1:
                w_of[t + 1], dn_of[t + 1], up_of[t + 1] = products(t + 1)
            for c in range(3):
                y = up_of[t + 1][c] + dn_of[t - 1][c]
                z = factor * (dinv[t, c] * y) - tk[k, t, c]
                tk[k + 2, t, c] = z
                if c < 2:
                    dz = dm[t, c] * z
                    odd[c] = odd[c] + dz * w_of[t][c]
                    even[c] = even[c] + dz * z
            dn_of.pop(t - 1), up_of.pop(t, None), w_of.pop(t)
        mom[2 * k + 1] = odd[0] + odd[1]
        mom[2 * k + 2] = even[0] + even[1]
        return carry

    lax.fori_loop(0, ITERS, power, 0)

    part = zero
    for n in range(2 * ITERS):
        part = jnp.where(sub == n, jnp.sum(mom[n], axis=0, keepdims=True), part)
    ar1[me_x] = part
    row_sum = [
        remote(ar1.at[me_x], ar1.at[me_x], sendr, recvr, o, peer(0, o)) for o in range(1, nx)
    ]
    for x in row_sum:
        x.start()
    for x in row_sum:
        x.wait_recv()
    part = sum_all(ar1, nx)
    ar2[me_y] = part
    col_sum = [
        remote(ar2.at[me_y], ar2.at[me_y], sendc, recvc, o, peer(o, 0)) for o in range(1, ny)
    ]
    for x in col_sum:
        x.start()
    for x in col_sum:
        x.wait_recv()
    whole = jnp.sum(sum_all(ar2, ny), axis=1, keepdims=True)
    raw = [jnp.broadcast_to(whole[n : n + 1, :], (SUB, LANES)) for n in range(2 * ITERS)]
    nu = [raw[0], raw[1]]
    for n in range(2, 2 * ITERS):
        nu.append(2.0 * raw[n] - nu[n % 2])
    c_p, c_z = scalars(nu)

    stores = []
    for n, out in ((0, out_p), (1, out_r)):
        for c in range(2):
            for t in range(T):
                if n == 0:
                    wet = lp[0, c, row_of(t), :] > 0.0
                    value = jnp.where(wet, lp[1, c, row_of(t), :], 0.0)
                    for m in range(ITERS):
                        value = value + c_p[m] * tk[m + 1, t, c]
                else:
                    value = c_z[0] * tk[1, t, c]
                    for m in range(1, ITERS + 1):
                        value = value + c_z[m] * tk[m + 1, t, c]
                    value = dm[t, c] * value
                ores[n, c, pl.ds(t, SUB, stride=T), :] = value
            stores.append(
                pltpu.make_async_copy(
                    ores.at[n, c, pl.ds(HALO, rows)],
                    out.at[:, pl.ds(c * LANES, LANES)],
                    out_sem.at[n, c],
                )
            )
            stores[-1].start()
    for x in first + second + row_sum + col_sum:
        x.wait_send()
    for x in stores:
        x.wait()


def sum_all(ref, count):
    parts = [ref[n] for n in range(count)]
    while len(parts) > 1:
        parts = [parts[n] + parts[n + 1] for n in range(0, len(parts), 2)]
    return parts[0]


def shards(ny, nx, fields, level_count, thickness, old_pressure):
    km, rows = fields.shape[1], fields.shape[2]
    ext = rows + 2 * HALO
    T = ext // SUB
    f32 = jnp.float32
    dma = pltpu.SemaphoreType.DMA
    vreg = (SUB, LANES)
    scratch = [
        pltpu.VMEM((3, km, 2, ext + 2 * PAD, LANES), f32),
        pltpu.VMEM((2, rows, LANES), jnp.int32),
        pltpu.VMEM((2, 3, ext + 2 * PAD, LANES), f32),
        pltpu.VMEM((2, 32, LANES), f32),
        pltpu.VMEM((2, 32, LANES), f32),
        pltpu.VMEM((4,) + vreg, f32),
        pltpu.VMEM((T, 3) + vreg, f32),
        pltpu.VMEM((3, ext, LANES), f32),
        pltpu.VMEM((3, ext, LANES), f32),
        pltpu.VMEM((2, 24, LANES), f32),
        pltpu.VMEM((2, 3, 16, LANES), f32),
        pltpu.VMEM((2, 24, LANES), f32),
        pltpu.VMEM((4,) + vreg, f32),
        pltpu.VMEM((T + 1, 3) + vreg, f32),
        pltpu.VMEM((T + 1, 3) + vreg, f32),
        pltpu.VMEM((T, 2) + vreg, f32),
        pltpu.VMEM((T, 3) + vreg, f32),
        pltpu.VMEM((T, 3) + vreg, f32),
        pltpu.VMEM((ITERS + 2, T, 3) + vreg, f32),
        pltpu.VMEM((2 * ITERS + 1,) + vreg, f32),
        pltpu.VMEM((nx,) + vreg, f32),
        pltpu.VMEM((ny,) + vreg, f32),
        pltpu.VMEM((2, 2, ext, LANES), f32),
        dma((4,)),
        dma((km, 2)),
        dma((8,)),
        dma((8,)),
        dma((8,)),
        dma((8,)),
        dma((nx,)),
        dma((nx,)),
        dma((ny,)),
        dma((ny,)),
        dma((2, 2)),
    ]
    shape = jax.ShapeDtypeStruct(old_pressure.shape, f32)
    anywhere = pl.BlockSpec(memory_space=pl.ANY)
    return pl.pallas_call(
        functools.partial(kernel, (ny, nx, km, rows)),
        out_shape=(shape, shape),
        in_specs=[pl.BlockSpec(memory_space=pltpu.SMEM), anywhere, anywhere, anywhere],
        out_specs=(anywhere, anywhere),
        scratch_shapes=scratch,
        compiler_params=pltpu.CompilerParams(
            collective_id=0, has_side_effects=True, vmem_limit_bytes=40 * 1024 * 1024
        ),
    )(thickness, fields, level_count, old_pressure)


def solution(mesh):
    ny, nx = mesh.shape["by"], mesh.shape["bx"]
    field = P("by", "bx")
    return jax.shard_map(
        functools.partial(shards, ny, nx),
        mesh=mesh,
        in_specs=(P(None, None, "by", "bx"), field, P(), field),
        out_specs=(field, field),
        check_vma=False,
    )
```

time: 295 us -> 50.8 us (0.17); the launches traced: 291 us -> 50.6 us
  blocking collectives: 107 us -> 0 us
  starting transfers between devices: 55.8 us -> 0 us
  other arithmetic: 49.1 us -> 0 us
  Pallas kernels: 0 us -> 43.2 us
  waiting for transfers between devices: 40.3 us -> 0 us
  local copies, waits for them, and re-layouts: 24 us -> 6.74 us
  between operations: 14.7 us -> 0.65 us
    psum x16 -> x0, blocking collectives: 107 us -> none  [over_axes(): array = lax.psum(array, axis)]
    ppermute x28 -> x0, starting transfers between devices: 55.8 us -> none  [the longest x14 28 us: padded(): before = lax.ppermute(last, axis, up)]
    pallas_call x0 -> x1, Pallas kernels: none -> 43.2 us  [shards(): pl.pallas_call(functools.partial(kernel, (ny, nx, km, rows)), out_shape=(...]
    ppermute x28 -> x0, waiting for transfers between devices: 40.3 us -> none  [the longest x14 27.6 us: padded(): before = lax.ppermute(last, axis, up)]
    sub x3 -> x0, other arithmetic: 24.4 us -> none  [the longest x1 17.4 us: level_divergence(): -VISCOSITY * laplace(laplace(zonal))]
    concatenate x12 -> x0, other arithmetic: 10.6 us -> none  [padded(): array = jnp.concatenate([before, array, after], axis=dim)]
    reduce_sum x5 -> x0, other arithmetic: 9.81 us -> none  [the longest x1 6.36 us: shards(): forcing_sum = jnp.sum(weights * level_divergence(extended), axis=0)]
    squeeze x1 -> x0, local copies, waits for them, and re-layouts: 6.08 us -> none  [level_divergence(): zonal = extended[0]]
  transfers between devices with their start and end apart: 28 -> 0, of which waited for: 17 -> 0; matrix products, arithmetic and copies ran while one was open for 20% -> 0% of each run, Pallas kernels for 0% -> 0%
where the time goes in v1:
time: 50.8 us; the launch traced here: 50.6 us
  Pallas kernels  43.2 us (85%)
  local copies, waits for them, and re-layouts  6.74 us (13%)
  between operations  0.65 us (1%)
    pallas_call x1, Pallas kernels, shards(): pl.pallas_call(functools.partial(kernel, (ny, nx, km, rows)), out_shape=(...  43.2 us
    unnamed x10, local copies, waits for them, and re-layouts  6.74 us

profile of v1, /device:TPU:1, one launch (start us, length us, event | category | flops | bytes accessed | tf_op | source)
XLA Modules:
  0.0 50.6 jit_solution(30017514079118279)
XLA Ops:
  0.6 0.0 copy-start
  0.6 2.8 %copy-done = f32[3,8,256,256]{3,2,1,0:T(8,128)S(1)} copy-done((f32[3,8,256,256]{3,2,1,0:T(8,128)S(1)}, f32[3,8,256,256]{3,2,1,0:T(8,128)}, u32[]{:S(2)}) %copy-start) | copy-done | bytes 6291480
  3.4 0.0 copy-start.1
  3.4 0.9 %copy-done.1 = s32[256,256]{1,0:T(8,128)S(1)} copy-done((s32[256,256]{1,0:T(8,128)S(1)}, s32[256,256]{1,0:T(8,128)}, u32[]{:S(2)}) %copy-start.1) | copy-done | bytes 262168
  4.4 0.0 copy-start.2
  4.4 0.9 %copy-done.2 = f32[256,256]{1,0:T(8,128)S(1)} copy-done((f32[256,256]{1,0:T(8,128)S(1)}, f32[256,256]{1,0:T(8,128)}, u32[]{:S(2)}) %copy-start.2) | copy-done | bytes 262168
  5.3 0.0 copy-start.3
  5.3 0.7 %copy-done.3 = f32[8]{0:T(128)S(1)} copy-done((f32[8]{0:T(128)S(1)}, f32[8]{0:T(128)}, u32[]{:S(2)}) %copy-start.3) | copy-done | bytes 56
  6.0 43.2 %shard_map.59 = (f32[256,256]{1,0:T(8,128)S(1)}, f32[256,256]{1,0:T(8,128)S(1)}) custom-call(f32[8]{0:T(128)S(1)} %copy-done.3, f32[3,8,256,256]{3,2,1,0:T(8,128)S(1)} %copy-done, s32[256,256]{1,0:T(8,128)S(1)} %copy-done.1, f32[256,256]{1,0:T(8,128)S(1)} %copy-done.2), custom_call_target="tpu_custom_call" | custom-call | tf_op jit(solution)/shard_map/pallas_call | solution.py:568
  49.2 0.7 %copy.8 = f32[256,256]{1,0:T(8,128)} copy(f32[256,256]{1,0:T(8,128)S(1)} %get-tuple-element.4) | data formatting | bytes 524288
  49.9 0.7 %copy.9 = f32[256,256]{1,0:T(8,128)} copy(f32[256,256]{1,0:T(8,128)S(1)} %get-tuple-element.5) | data formatting | bytes 524288
Async XLA Ops:
  0.6 2.8 %copy-start = (f32[3,8,256,256]{3,2,1,0:T(8,128)S(1)}, f32[3,8,256,256]{3,2,1,0:T(8,128)}, u32[]{:S(2)}) copy-start(f32[3,8,256,256]{3,2,1,0:T(8,128)} %fields.1) | copy-start | bytes 18874372
  3.4 0.9 %copy-start.1 = (s32[256,256]{1,0:T(8,128)S(1)}, s32[256,256]{1,0:T(8,128)}, u32[]{:S(2)}) copy-start(s32[256,256]{1,0:T(8,128)} %level_count.1) | copy-start | bytes 786436
  4.4 0.9 %copy-start.2 = (f32[256,256]{1,0:T(8,128)S(1)}, f32[256,256]{1,0:T(8,128)}, u32[]{:S(2)}) copy-start(f32[256,256]{1,0:T(8,128)} %old_pressure.1) | copy-start | bytes 786436
  5.3 0.7 %copy-start.3 = (f32[8]{0:T(128)S(1)}, f32[8]{0:T(128)}, u32[]{:S(2)}) copy-start(f32[8]{0:T(128)} %th.1) | copy-start | bytes 100

commit v2 on v1

--- a/solution.py
+++ b/solution.py
@@ -10,6 +10,9 @@
 VISCOSITY = 0.05
 IMPLICIT = 0.05
 ITERS = 4
+STEPS = 38
+UNROLL = 19
+REACH = 3
 MESH = pl.DeviceIdType.MESH
 
 LANES = 128
@@ -23,7 +26,17 @@
 
 
 def roll(x, shift):
-    return pltpu.roll(x, shift % LANES, axis=1)
+    shift = shift % LANES if isinstance(shift, int) else lax.rem(shift + 2 * LANES, LANES)
+    return pltpu.roll(x, shift, axis=1)
+
+
+def steps(count, unroll, body, carry=()):
+    def chunk(n, carry):
+        for m in range(unroll):
+            carry = body(n * unroll + m, carry)
+        return carry
+
+    return lax.fori_loop(0, count // unroll, chunk, carry)
 
 
 def from_east(tiles, lane, by=1):
@@ -105,8 +118,7 @@
     fields,
     level_count,
     old_pressure,
-    out_p,
-    out_r,
+    ores,
     fb,
     lev,
     lp,
@@ -114,6 +126,7 @@
     got1,
     got1d,
     fv,
+    lcs,
     fr,
     ft,
     fold,
@@ -129,7 +142,6 @@
     mom,
     ar1,
     ar2,
-    ores,
     load_sem,
     field_sem,
     send1,
@@ -140,12 +152,11 @@
     recvr,
     sendc,
     recvc,
-    out_sem,
 ):
     ny, nx, km, rows = dims
     ext = rows + 2 * HALO
     T = ext // SUB
-    own = rows // SUB
+    before = STEPS - T
     me_y, me_x = lax.axis_index("by"), lax.axis_index("bx")
     lane = lane_ids()
     sub = lax.broadcasted_iota(jnp.int32, (SUB, LANES), 0)
@@ -196,30 +207,42 @@
             lp[n, c, pl.ds(0, SUB), :] = zero
             lp[n, c, pl.ds(ext + PAD, SUB), :] = zero
 
+    for c in range(3):
+        for r in range(T, T + 2):
+            fr[c, pl.ds(r * SUB, SUB), :] = zero
+
     def clear_sum(t, carry):
         for c in range(3):
-            fv[t, c] = zero
             tk[0, t, c] = zero
-        return carry
-
-    lax.fori_loop(0, T, clear_sum, 0)
+        for m in range(2 * REACH + 1):
+            for c in range(2):
+                fv[m, t + before, c] = zero
+        return carry
+
+    steps(T, 2, clear_sum, 0)
 
     for x in loads:
         x.wait()
-    packed = [[zero] * 4, [zero] * 4]
-    for r in range(own):
-        at = pl.ds(PAD + HALO + r * SUB, SUB)
-        group, pos = r % 8, r // 8
+
+    def pack_group(group, carry):
         mask = (lane >= 16 * group) & (lane < 16 * group + 16)
-        for c in range(2):
-            lp[0, c, at, :] = lev[c, pl.ds(r * SUB, SUB), :].astype(jnp.float32)
-        east = jnp.where(lane >= 120, lp[0, 1, at, :], roll(lp[1, 1, at, :], -8))
-        west = jnp.where(lane < 8, lp[0, 0, at, :], roll(lp[1, 0, at, :], 8))
-        packed[0][pos] = jnp.where(mask, roll(east, 16 * group + 16), packed[0][pos])
-        packed[1][pos] = jnp.where(mask, roll(west, 16 * group), packed[1][pos])
+        out = []
+        for pos in range(4):
+            row = pl.multiple_of((pos * 8 + group) * SUB, SUB)
+            at = pl.ds(PAD + HALO + row, SUB)
+            count = [lev[c, pl.ds(row, SUB), :].astype(jnp.float32) for c in range(2)]
+            for c in range(2):
+                lp[0, c, at, :] = count[c]
+            east = jnp.where(lane >= 120, count[1], roll(lp[1, 1, at, :], -8))
+            west = jnp.where(lane < 8, count[0], roll(lp[1, 0, at, :], 8))
+            out.append(jnp.where(mask, roll(east, 16 * group + 16), carry[2 * pos]))
+            out.append(jnp.where(mask, roll(west, 16 * group), carry[2 * pos + 1]))
+        return tuple(out)
+
+    packed = steps(8, 2, pack_group, (zero,) * 8)
     for side in range(2):
         for pos in range(4):
-            pack[side, pl.ds(pos * SUB, SUB), :] = packed[side][pos]
+            pack[side, pl.ds(pos * SUB, SUB), :] = packed[2 * pos + side]
     pl.semaphore_wait(barrier, len(peers))
 
     def remote(src, dst, send, recv, n, target):
@@ -257,78 +280,113 @@
         lp[0, 2, at, :] = jnp.where(lane < 64, lev_e, lev_w)
         lp[1, 2, at, :] = jnp.where(lane < 64, old_e, old_w)
 
-    for r in range(own):
-        row = pl.ds((r // 8) * SUB, SUB)
-        place(pl.ds(low + r * SUB, SUB), got1[0, row, :], got1[1, row, :], r % 8)
+    def unpack_group(group, carry):
+        for pos in range(4):
+            row = pl.ds(pos * SUB, SUB)
+            at = pl.ds(low + pl.multiple_of((pos * 8 + group) * SUB, SUB), SUB)
+            place(at, got1[0, row, :], got1[1, row, :], group)
+        return carry
+
+    steps(8, 2, unpack_group, 0)
     place(pl.ds(PAD, SUB), got1d[0], got1d[1], 7)
     place(pl.ds(high + SUB, SUB), got1d[2], got1d[3], 0)
 
     def row_of(t):
         return pl.ds(t + PAD, SUB, stride=T)
+
+    def shift_counts(group, carry):
+        words = []
+        for c in range(3):
+            word = None
+            for r in range(7):
+                count = lp[0, c, row_of(group * 7 + r), :].astype(jnp.int32)
+                word = count if r == 0 else word | (count << (4 * r))
+            words.append(word)
+        for m in range(-REACH, REACH + 1):
+            moved = words
+            if m > 0:
+                moved = from_west(words, lane, m)
+            elif m < 0:
+                moved = from_east(words, lane, -m)
+            for c in range(2):
+                for r in range(7):
+                    lcs[m + REACH, group * 7 + r + before, c] = (moved[c] >> (4 * r)) & 15
+        return carry
+
+    steps(-(-T // 7), 1, shift_counts, 0)
 
     def level(k, carry):
         for c in range(2):
             field_copy(k, c).wait()
-        weight = th[k] * (-0.5 * VISCOSITY)
-        here = k.astype(jnp.float32)
-        u, v, p, g, h = {}, {}, {}, {}, {}
+        scale = th[k] * (-0.5 * VISCOSITY)
+        scale_u = 2.0 * scale
+        scale_p = (0.5 / VISCOSITY) * scale
 
         def load(f, t):
             return [fb[f, k, c, row_of(t), :] for c in range(2)]
 
-        for step in range(-3, T + 3):
-            v[step] = load(1, step)
-            t = step - 1
-            if -2 <= t:
-                w = load(0, t) + [None]
-                e, o = from_east(w, lane), from_west(w, lane)
-                g[t] = [
-                    (e[0] - o[0]) + (v[t + 1][0] - v[t - 1][0]),
-                    (e[1] - o[1]) + (v[t + 1][1] - v[t - 1][1]),
-                    e[2] - o[2],
-                ]
-                p[t] = load(2, t)
-                v.pop(t - 1)
-            t = step - 2
-            if -1 <= t:
-                e, o = from_east(g[t], lane), from_west(g[t], lane)
-                h[t] = [
-                    (e[c] + o[c]) + (g[t + 1][c] + g[t - 1][c]) - 4.0 * g[t][c] for c in range(3)
-                ]
-                g.pop(t - 1)
-            t = step - 3
-            if 0 <= t:
-                e, o = from_east(h[t], lane), from_west(h[t], lane)
-                ee, oo = from_east(p[t] + [None], lane, 2), from_west(p[t] + [None], lane, 2)
-                for c in range(3):
-                    bi = (e[c] + o[c]) + (h[t + 1][c] + h[t - 1][c]) - 4.0 * h[t][c]
-                    pr = ee[c] + oo[c]
-                    if c < 2:
-                        pr = pr + (p[t + 2][c] + p[t - 2][c]) - 4.0 * p[t][c]
-                    term = bi + (0.5 / VISCOSITY) * pr
-                    wet = jnp.where(lp[0, c, row_of(t), :] > here, weight, 0.0)
-                    fv[t, c] += wet * term
-                h.pop(t - 1)
-                p.pop(t - 2)
+        def row_step(n, carry):
+            t = n - before
+            u0, u1, a0, a1, v0, v1, e0, e1, p0, p1, p2, p3 = carry
+            u2, p4 = load(0, t + 2), load(2, t + 2)
+            north, south = load(1, t + 3), load(1, t + 1)
+            out = [[] for _ in carry]
+            for c in range(2):
+                u2_ = u2[c] * scale_u
+                p4_ = p4[c] * scale_p
+                v2 = (north[c] - south[c]) * scale
+                a2 = (u2_ + u0[c]) - 4.0 * u1[c]
+                e2 = (v2 + v0[c]) - 4.0 * v1[c]
+                b = v0[c] + p2[c]
+                d = 4.0 * e1[c]
+                odd = u0[c] + ((a2 + a0[c]) - 4.0 * a1[c])
+                here = ((e2 + e0[c]) + (p4_ + p0[c])) - 4.0 * (e1[c] + p2[c]) + (v0[c] + v0[c])
+                terms = [None, b - a1[c], d - odd, here, d + odd, b + a1[c], u0[c]]
+                for m, term in enumerate(terms):
+                    wet = lcs[m, n, c] > k
+                    if m == 0:
+                        fv[m, n, c] -= jnp.where(wet, u0[c], 0.0)
+                    else:
+                        fv[m, n, c] += jnp.where(wet, term, 0.0)
+                row = (u1[c], u2_, a1[c], a2, v1[c], v2, e1[c], e2, p1[c], p2[c], p3[c], p4_)
+                for x, y in zip(out, row):
+                    x.append(y)
+            return tuple(out)
+
+        steps(STEPS, UNROLL, row_step, ([zero] * 2,) * 12)
         return carry
 
     lax.fori_loop(0, km, level, 0)
 
-    for t in range(T):
+    def to_rows(t, carry):
+        tiles = [[fv[m, t + before, c] for c in range(2)] + [None] for m in range(2 * REACH + 1)]
+        total = [tiles[REACH][0], tiles[REACH][1], 0.0]
+        for m in range(1, REACH + 1):
+            scale = 1.0 if m == 2 else 0.5
+            e = from_east(tiles[REACH + m], lane, m)
+            o = from_west(tiles[REACH - m], lane, m)
+            total = [total[c] + scale * (e[c] + o[c]) for c in range(3)]
         for c in range(3):
-            fr[c, pl.ds(t, SUB, stride=T), :] = fv[t, c]
-    folded = [[zero] * 3, [zero] * 3]
-    for r in range(T):
-        at = pl.ds(r * SUB, SUB)
-        group, pos = r % 12, r // 12
+            fr[c, pl.ds(t, SUB, stride=T), :] = total[c]
+        return carry
+
+    steps(T, 2, to_rows, 0)
+
+    def fold_group(group, carry):
         mask = (lane >= 8 * group) & (lane < 8 * group + 8)
-        east = roll(jnp.where(lane < 64, fr[2, at, :], fr[1, at, :]), 4 + 8 * group)
-        west = roll(jnp.where(lane < 64, fr[0, at, :], fr[2, at, :]), 4 + 8 * group)
-        folded[0][pos] = jnp.where(mask, east, folded[0][pos])
-        folded[1][pos] = jnp.where(mask, west, folded[1][pos])
+        out = []
+        for pos in range(3):
+            at = pl.ds(pl.multiple_of((pos * 12 + group) * SUB, SUB), SUB)
+            east = roll(jnp.where(lane < 64, fr[2, at, :], fr[1, at, :]), 4 + 8 * group)
+            west = roll(jnp.where(lane < 64, fr[0, at, :], fr[2, at, :]), 4 + 8 * group)
+            out.append(jnp.where(mask, east, carry[2 * pos]))
+            out.append(jnp.where(mask, west, carry[2 * pos + 1]))
+        return tuple(out)
+
+    folded = steps(12, 2, fold_group, (zero,) * 6)
     for side in range(2):
         for pos in range(3):
-            fold[side, pl.ds(pos * SUB, SUB), :] = folded[side][pos]
+            fold[side, pl.ds(pos * SUB, SUB), :] = folded[2 * pos + side]
     second = [
         remote(fr.at[:, pl.ds(ext - 16, 16)], got2y.at[0], send2, recv2, 0, peer(1, 0)),
         remote(fr.at[:, pl.ds(0, 16)], got2y.at[1], send2, recv2, 1, peer(-1, 0)),
@@ -355,72 +413,72 @@
     def guess_of(t):
         return [jnp.where(lp[0, c, row_of(t), :] > 0.0, lp[1, c, row_of(t), :], 0.0) for c in range(3)]
 
-    depth, mid, west, up, down = {-1: depth_of(-1)}, {}, {}, {}, {}
-    for step in range(-1, T + 1):
-        t = step
-        if t < T:
-            depth[t + 1] = depth_of(t + 1)
-            low2 = [jnp.minimum(depth[t][c], depth[t + 1][c]) for c in range(3)]
-            e = from_east(low2, lane)
-            mid[t] = [0.5 * jnp.minimum(low2[c], e[c]) for c in range(3)]
-            west[t] = from_west(mid[t], lane)
-            depth.pop(t)
-            for c in range(3):
-                c00[t + 1, c] = mid[t][c]
-                c0m[t + 1, c] = west[t][c]
-        guess = guess_of(t)
-        e, o = from_east(guess, lane), from_west(guess, lane)
-        if t < T:
-            down[t] = [mid[t][c] * e[c] + west[t][c] * o[c] for c in range(3)]
-        if t >= 0:
-            up[t] = [mid[t - 1][c] * e[c] + west[t - 1][c] * o[c] for c in range(3)]
-        t = step - 1
-        if t >= 0:
-            guess = guess_of(t)
-            for c in range(3):
-                k_sum = (mid[t][c] + mid[t - 1][c]) + (west[t][c] + west[t - 1][c])
-                diagonal = IMPLICIT + k_sum
-                dinv[t, c] = 1.0 / diagonal
-                q0[t, c] = (up[t + 1][c] + down[t - 1][c]) - k_sum * guess[c]
-                if c < 2:
-                    if t < HALO:
-                        diagonal = jnp.where(sub == 0, 0.0, diagonal)
-                    if t >= T - HALO:
-                        diagonal = jnp.where(sub == SUB - 1, 0.0, diagonal)
-                    dm[t, c] = diagonal
-            mid.pop(t - 1), west.pop(t - 1), up.pop(t, None), down.pop(t - 1)
+    def coefficient_step(n, carry):
+        t = n - 1
+        depth0, mid0, west0, down0, down1, k0, guess0 = carry
+        depth1 = depth_of(t + 1)
+        low2 = [jnp.minimum(depth0[c], depth1[c]) for c in range(3)]
+        e = from_east(low2, lane)
+        mid1 = [0.5 * jnp.minimum(low2[c], e[c]) for c in range(3)]
+        west1 = from_west(mid1, lane)
+        guess1 = guess_of(t)
+        e, o = from_east(guess1, lane), from_west(guess1, lane)
+        down2 = [mid1[c] * e[c] + west1[c] * o[c] for c in range(3)]
+        k1 = [(mid1[c] + mid0[c]) + (west1[c] + west0[c]) for c in range(3)]
+        outside = ((sub == 0) & (t - 1 < HALO)) | ((sub == SUB - 1) & (t - 1 >= T - HALO))
+        for c in range(3):
+            c00[n, c] = mid1[c]
+            c0m[n, c] = west1[c]
+            up = mid0[c] * e[c] + west0[c] * o[c]
+            diagonal = IMPLICIT + k0[c]
+            dinv[n, c] = 1.0 / diagonal
+            q0[n, c] = (up + down0[c]) - k0[c] * guess0[c]
+            if c < 2:
+                dm[n, c] = jnp.where(outside, 0.0, diagonal)
+        return depth1, mid1, west1, down1, down2, k1, guess1
+
+    steps(T + 2, 4, coefficient_step, (depth_of(-1),) + ([zero] * 3,) * 6)
 
     for x in second:
         x.wait_recv()
-    for r in range(T):
-        at = pl.ds(r * SUB, SUB)
-        group, pos = r % 12, pl.ds((r // 12) * SUB, SUB)
-        shift = -(4 + 8 * group)
-        east = roll(got2x[0, pos, :], shift)
-        west_ = roll(got2x[1, pos, :], shift)
-        total = [fr[c, at, :] for c in range(3)]
-        if r < 2:
-            total = [total[c] + got2y[0, c, at, :] for c in range(3)]
-            east = east + roll(got2d[0], -(4 + 8 * (8 + r)))
-            west_ = west_ + roll(got2d[1], -(4 + 8 * (8 + r)))
-        if r >= T - 2:
-            row = pl.ds((r - T + 2) * SUB, SUB)
-            total = [total[c] + got2y[1, c, row, :] for c in range(3)]
-            east = east + roll(got2d[2], -(4 + 8 * (r - T + 2)))
-            west_ = west_ + roll(got2d[3], -(4 + 8 * (r - T + 2)))
-        ft[0, at, :] = total[0] + jnp.where(lane < 4, east, 0.0)
-        ft[1, at, :] = total[1] + jnp.where(lane >= 124, west_, 0.0)
-        ft[2, at, :] = total[2] + jnp.where(lane < 4, west_, jnp.where(lane >= 124, east, 0.0))
-
-    acc = [zero, zero]
-    for t in range(T):
+
+    def gather_group(group, carry):
+        for pos in range(3):
+            at = pl.ds(pl.multiple_of((pos * 12 + group) * SUB, SUB), SUB)
+            row = pl.ds(pos * SUB, SUB)
+            east = roll(got2x[0, row, :], -(4 + 8 * group))
+            west = roll(got2x[1, row, :], -(4 + 8 * group))
+            ft[0, at, :] = fr[0, at, :] + jnp.where(lane < 4, east, 0.0)
+            ft[1, at, :] = fr[1, at, :] + jnp.where(lane >= 124, west, 0.0)
+            ft[2, at, :] = fr[2, at, :] + jnp.where(lane < 4, west, jnp.where(lane >= 124, east, 0.0))
+        return carry
+
+    steps(12, 2, gather_group, 0)
+    for n in range(2):
+        for side in range(2):
+            row = pl.ds(n * SUB, SUB)
+            at = pl.ds((T - 2 + n if side else n) * SUB, SUB)
+            shift = -(4 + 8 * (n if side else 8 + n))
+            east = roll(got2d[2 * side], shift)
+            west = roll(got2d[2 * side + 1], shift)
+            ft[0, at, :] += got2y[side, 0, row, :] + jnp.where(lane < 4, east, 0.0)
+            ft[1, at, :] += got2y[side, 1, row, :] + jnp.where(lane >= 124, west, 0.0)
+            ft[2, at, :] += got2y[side, 2, row, :] + jnp.where(
+                lane < 4, west, jnp.where(lane >= 124, east, 0.0)
+            )
+
+    def residual_step(t, carry):
+        out = []
         for c in range(3):
             force = ft[c, pl.ds(t, SUB, stride=T), :]
             wet = lp[0, c, row_of(t), :] > 0.0
-            z = (jnp.where(wet, force, 0.0) + q0[t, c]) * dinv[t, c]
+            z = (jnp.where(wet, force, 0.0) + q0[t + 2, c]) * dinv[t + 2, c]
             tk[1, t, c] = z
             if c < 2:
-                acc[c] = acc[c] + (dm[t, c] * z) * z
+                out.append(carry[c] + (dm[t + 2, c] * z) * z)
+        return tuple(out)
+
+    acc = steps(T, 2, residual_step, (zero, zero))
     mom[0] = acc[0] + acc[1]
 
     def power(k, carry):
@@ -444,10 +502,10 @@
                 w_of[t + 1], dn_of[t + 1], up_of[t + 1] = products(t + 1)
             for c in range(3):
                 y = up_of[t + 1][c] + dn_of[t - 1][c]
-                z = factor * (dinv[t, c] * y) - tk[k, t, c]
+                z = factor * (dinv[t + 2, c] * y) - tk[k, t, c]
                 tk[k + 2, t, c] = z
                 if c < 2:
-                    dz = dm[t, c] * z
+                    dz = dm[t + 2, c] * z
                     odd[c] = odd[c] + dz * w_of[t][c]
                     even[c] = even[c] + dz * z
             dn_of.pop(t - 1), up_of.pop(t, None), w_of.pop(t)
@@ -484,31 +542,35 @@
         nu.append(2.0 * raw[n] - nu[n % 2])
     c_p, c_z = scalars(nu)
 
-    stores = []
-    for n, out in ((0, out_p), (1, out_r)):
+    def output_step(t, carry):
         for c in range(2):
-            for t in range(T):
-                if n == 0:
-                    wet = lp[0, c, row_of(t), :] > 0.0
-                    value = jnp.where(wet, lp[1, c, row_of(t), :], 0.0)
-                    for m in range(ITERS):
-                        value = value + c_p[m] * tk[m + 1, t, c]
-                else:
-                    value = c_z[0] * tk[1, t, c]
-                    for m in range(1, ITERS + 1):
-                        value = value + c_z[m] * tk[m + 1, t, c]
-                    value = dm[t, c] * value
-                ores[n, c, pl.ds(t, SUB, stride=T), :] = value
-            stores.append(
-                pltpu.make_async_copy(
-                    ores.at[n, c, pl.ds(HALO, rows)],
-                    out.at[:, pl.ds(c * LANES, LANES)],
-                    out_sem.at[n, c],
-                )
-            )
-            stores[-1].start()
+            z = [tk[m + 1, t, c] for m in range(ITERS + 1)]
+            wet = lp[0, c, row_of(t), :] > 0.0
+            value = jnp.where(wet, lp[1, c, row_of(t), :], 0.0)
+            for m in range(ITERS):
+                value = value + c_p[m] * z[m]
+            ores[0, c, pl.ds(t, SUB, stride=T), :] = value
+            value = c_z[0] * z[0]
+            for m in range(1, ITERS + 1):
+                value = value + c_z[m] * z[m]
+            ores[1, c, pl.ds(t, SUB, stride=T), :] = dm[t + 2, c] * value
+        return carry
+
+    steps(T, 2, output_step, 0)
     for x in first + second + row_sum + col_sum:
         x.wait_send()
+
+
+def write_out(rows, ores, out_p, out_r, sem):
+    stores = [
+        pltpu.make_async_copy(
+            ores.at[n, c, pl.ds(HALO, rows)], out.at[:, pl.ds(c * LANES, LANES)], sem.at[n, c]
+        )
+        for n, out in ((0, out_p), (1, out_r))
+        for c in range(2)
+    ]
+    for x in stores:
+        x.start()
     for x in stores:
         x.wait()
 
@@ -534,23 +596,23 @@
         pltpu.VMEM((2, 32, LANES), f32),
         pltpu.VMEM((2, 32, LANES), f32),
         pltpu.VMEM((4,) + vreg, f32),
-        pltpu.VMEM((T, 3) + vreg, f32),
-        pltpu.VMEM((3, ext, LANES), f32),
-        pltpu.VMEM((3, ext, LANES), f32),
+        pltpu.VMEM((2 * REACH + 1, STEPS, 2) + vreg, f32),
+        pltpu.VMEM((2 * REACH + 1, STEPS + 1, 2) + vreg, jnp.int32),
+        pltpu.VMEM((3, ext + 2 * SUB, LANES), f32),
+        pltpu.VMEM((3, ext + 2 * SUB, LANES), f32),
         pltpu.VMEM((2, 24, LANES), f32),
         pltpu.VMEM((2, 3, 16, LANES), f32),
         pltpu.VMEM((2, 24, LANES), f32),
         pltpu.VMEM((4,) + vreg, f32),
-        pltpu.VMEM((T + 1, 3) + vreg, f32),
-        pltpu.VMEM((T + 1, 3) + vreg, f32),
-        pltpu.VMEM((T, 2) + vreg, f32),
-        pltpu.VMEM((T, 3) + vreg, f32),
-        pltpu.VMEM((T, 3) + vreg, f32),
+        pltpu.VMEM((T + 2, 3) + vreg, f32),
+        pltpu.VMEM((T + 2, 3) + vreg, f32),
+        pltpu.VMEM((T + 2, 2) + vreg, f32),
+        pltpu.VMEM((T + 2, 3) + vreg, f32),
+        pltpu.VMEM((T + 2, 3) + vreg, f32),
         pltpu.VMEM((ITERS + 2, T, 3) + vreg, f32),
         pltpu.VMEM((2 * ITERS + 1,) + vreg, f32),
         pltpu.VMEM((nx,) + vreg, f32),
         pltpu.VMEM((ny,) + vreg, f32),
-        pltpu.VMEM((2, 2, ext, LANES), f32),
         dma((4,)),
         dma((km, 2)),
         dma((8,)),
@@ -561,20 +623,28 @@
         dma((nx,)),
         dma((ny,)),
         dma((ny,)),
-        dma((2, 2)),
     ]
-    shape = jax.ShapeDtypeStruct(old_pressure.shape, f32)
-    anywhere = pl.BlockSpec(memory_space=pl.ANY)
-    return pl.pallas_call(
+    hbm = pl.BlockSpec(memory_space=pltpu.HBM)
+    vmem = pl.BlockSpec(memory_space=pltpu.VMEM)
+    result = pl.pallas_call(
         functools.partial(kernel, (ny, nx, km, rows)),
-        out_shape=(shape, shape),
-        in_specs=[pl.BlockSpec(memory_space=pltpu.SMEM), anywhere, anywhere, anywhere],
-        out_specs=(anywhere, anywhere),
+        out_shape=pltpu.VMEM((2, 2, ext, LANES), f32),
+        in_specs=[pl.BlockSpec(memory_space=pltpu.SMEM), hbm, hbm, hbm],
+        out_specs=vmem,
         scratch_shapes=scratch,
         compiler_params=pltpu.CompilerParams(
-            collective_id=0, has_side_effects=True, vmem_limit_bytes=40 * 1024 * 1024
+            collective_id=0, has_side_effects=True, vmem_limit_bytes=58 * 1024 * 1024
         ),
     )(thickness, fields, level_count, old_pressure)
+    shape = jax.ShapeDtypeStruct(old_pressure.shape, f32)
+    return pl.pallas_call(
+        functools.partial(write_out, rows),
+        out_shape=(shape, shape),
+        in_specs=[pl.BlockSpec(memory_space=pl.ANY)],
+        out_specs=(hbm, hbm),
+        scratch_shapes=[dma((2, 2))],
+        compiler_params=pltpu.CompilerParams(vmem_limit_bytes=4 * 1024 * 1024),
+    )(result)
 
 
 def solution(mesh):

time: 50.8 us -> 38.2 us (0.75)
  local copies, waits for them, and re-layouts: 6.74 us -> 0 us
  Pallas kernels: 43.2 us -> 37.5 us
    unnamed x10 -> x0, local copies, waits for them, and re-layouts: 6.74 us -> none
    pallas_call x1 -> x2, Pallas kernels: 43.2 us -> 37.5 us  [the longest x1 36.7 us: shards(): pl.pallas_call(functools.partial(kernel, (ny, nx, km, rows)), out_shape=p...]
where the time goes in v2:
time: 38.2 us; the launch traced here: 38.1 us
  Pallas kernels  37.5 us (98%)
  between operations  0.64 us (2%)
    pallas_call x1, Pallas kernels, shards(): pl.pallas_call(functools.partial(kernel, (ny, nx, km, rows)), out_shape=p...  36.7 us
    pallas_call x1, Pallas kernels, shards(): pl.pallas_call(functools.partial(write_out, rows), out_shape=(shape, shap...  0.82 us

profile of v2, /device:TPU:1, one launch (start us, length us, event | category | flops | bytes accessed | tf_op | source)
XLA Modules:
  0.0 38.1 jit_solution(462421581262554759)
XLA Ops:
  0.6 36.7 %shard_map.59.ores = f32[2,2,272,128]{3,2,1,0:T(8,128)S(1)} custom-call(f32[8]{0:T(128)} %th.1, f32[3,8,256,256]{3,2,1,0:T(8,128)} %fields.1, s32[256,256]{1,0:T(8,128)} %level_count.1, f32[256,256]{1,0:T(8,128)} %old_pressure.1), custom_call_target="tpu_custom_call" | custom-call | tf_op jit(solution)/shard_map/pallas_call | solution.py:629
  37.3 0.8 %shard_map.60 = (f32[256,256]{1,0:T(8,128)}, f32[256,256]{1,0:T(8,128)}) custom-call(f32[2,2,272,128]{3,2,1,0:T(8,128)S(1)} %shard_map.59.ores), custom_call_target="tpu_custom_call" | custom-call | tf_op jit(solution)/shard_map/pallas_call | solution.py:640

commit v3 on v2

--- a/solution.py
+++ b/solution.py
@@ -12,6 +12,7 @@
 ITERS = 4
 STEPS = 38
 UNROLL = 19
+UNROLL_SUM = 2
 REACH = 3
 MESH = pl.DeviceIdType.MESH
 
@@ -125,7 +126,7 @@
     pack,
     got1,
     got1d,
-    fv,
+    terms,
     lcs,
     fr,
     ft,
@@ -214,9 +215,6 @@
     def clear_sum(t, carry):
         for c in range(3):
             tk[0, t, c] = zero
-        for m in range(2 * REACH + 1):
-            for c in range(2):
-                fv[m, t + before, c] = zero
         return carry
 
     steps(T, 2, clear_sum, 0)
@@ -269,6 +267,47 @@
     ]
     for x in first:
         x.start()
+    def row_of(t):
+        return pl.ds(t + PAD, SUB, stride=T)
+
+    def level(k, carry):
+        for c in range(2):
+            field_copy(k, c).wait()
+        scale = th[k] * (-0.5 * VISCOSITY)
+        scale_u = 2.0 * scale
+        scale_p = (0.5 / VISCOSITY) * scale
+
+        def load(f, t):
+            return [fb[f, k, c, row_of(t), :] for c in range(2)]
+
+        def row_step(n, carry):
+            t = n - before
+            u0, u1, a0, a1, v0, v1, e0, e1, p0, p1, p2, p3 = carry
+            u2, p4 = load(0, t + 2), load(2, t + 2)
+            north, south = load(1, t + 3), load(1, t + 1)
+            out = [[] for _ in carry]
+            for c in range(2):
+                u2_ = u2[c] * scale_u
+                p4_ = p4[c] * scale_p
+                v2 = (north[c] - south[c]) * scale
+                a2 = (u2_ + u0[c]) - 4.0 * u1[c]
+                e2 = (v2 + v0[c]) - 4.0 * v1[c]
+                b = v0[c] + p2[c]
+                d = 4.0 * e1[c]
+                odd = u0[c] + ((a2 + a0[c]) - 4.0 * a1[c])
+                here = ((e2 + e0[c]) + (p4_ + p0[c])) - 4.0 * (e1[c] + p2[c]) + (v0[c] + v0[c])
+                for m, term in enumerate([u0[c], b - a1[c], d - odd, here, d + odd, b + a1[c]]):
+                    terms[k, n, m, c] = term
+                row = (u1[c], u2_, a1[c], a2, v1[c], v2, e1[c], e2, p1[c], p2[c], p3[c], p4_)
+                for x, y in zip(out, row):
+                    x.append(y)
+            return tuple(out)
+
+        steps(STEPS, UNROLL, row_step, ([zero] * 2,) * 12)
+        return carry
+
+    lax.fori_loop(0, km, level, 0)
+
     for x in first:
         x.wait_recv()
 
@@ -290,9 +329,6 @@
     steps(8, 2, unpack_group, 0)
     place(pl.ds(PAD, SUB), got1d[0], got1d[1], 7)
     place(pl.ds(high + SUB, SUB), got1d[2], got1d[3], 0)
-
-    def row_of(t):
-        return pl.ds(t + PAD, SUB, stride=T)
 
     def shift_counts(group, carry):
         words = []
@@ -310,67 +346,35 @@
                 moved = from_east(words, lane, -m)
             for c in range(2):
                 for r in range(7):
-                    lcs[m + REACH, group * 7 + r + before, c] = (moved[c] >> (4 * r)) & 15
+                    lcs[group * 7 + r, m + REACH, c] = (moved[c] >> (4 * r)) & 15
         return carry
 
     steps(-(-T // 7), 1, shift_counts, 0)
 
-    def level(k, carry):
-        for c in range(2):
-            field_copy(k, c).wait()
-        scale = th[k] * (-0.5 * VISCOSITY)
-        scale_u = 2.0 * scale
-        scale_p = (0.5 / VISCOSITY) * scale
-
-        def load(f, t):
-            return [fb[f, k, c, row_of(t), :] for c in range(2)]
-
-        def row_step(n, carry):
-            t = n - before
-            u0, u1, a0, a1, v0, v1, e0, e1, p0, p1, p2, p3 = carry
-            u2, p4 = load(0, t + 2), load(2, t + 2)
-            north, south = load(1, t + 3), load(1, t + 1)
-            out = [[] for _ in carry]
+    def to_rows(t, carry):
+        tiles = []
+        for m in range(2 * REACH + 1):
+            sums = []
             for c in range(2):
-                u2_ = u2[c] * scale_u
-                p4_ = p4[c] * scale_p
-                v2 = (north[c] - south[c]) * scale
-                a2 = (u2_ + u0[c]) - 4.0 * u1[c]
-                e2 = (v2 + v0[c]) - 4.0 * v1[c]
-                b = v0[c] + p2[c]
-                d = 4.0 * e1[c]
-                odd = u0[c] + ((a2 + a0[c]) - 4.0 * a1[c])
-                here = ((e2 + e0[c]) + (p4_ + p0[c])) - 4.0 * (e1[c] + p2[c]) + (v0[c] + v0[c])
-                terms = [None, b - a1[c], d - odd, here, d + odd, b + a1[c], u0[c]]
-                for m, term in enumerate(terms):
-                    wet = lcs[m, n, c] > k
-                    if m == 0:
-                        fv[m, n, c] -= jnp.where(wet, u0[c], 0.0)
-                    else:
-                        fv[m, n, c] += jnp.where(wet, term, 0.0)
-                row = (u1[c], u2_, a1[c], a2, v1[c], v2, e1[c], e2, p1[c], p2[c], p3[c], p4_)
-                for x, y in zip(out, row):
-                    x.append(y)
-            return tuple(out)
-
-        steps(STEPS, UNROLL, row_step, ([zero] * 2,) * 12)
-        return carry
-
-    lax.fori_loop(0, km, level, 0)
-
-    def to_rows(t, carry):
-        tiles = [[fv[m, t + before, c] for c in range(2)] + [None] for m in range(2 * REACH + 1)]
+                count = lcs[t, m, c]
+                total = None
+                for k in range(km):
+                    term = jnp.where(count > k, terms[k, t + before, m % (2 * REACH), c], 0.0)
+                    total = term if k == 0 else total + term
+                sums.append(total)
+            tiles.append(sums + [None])
         total = [tiles[REACH][0], tiles[REACH][1], 0.0]
         for m in range(1, REACH + 1):
-            scale = 1.0 if m == 2 else 0.5
             e = from_east(tiles[REACH + m], lane, m)
             o = from_west(tiles[REACH - m], lane, m)
-            total = [total[c] + scale * (e[c] + o[c]) for c in range(3)]
+            for c in range(3):
+                both = e[c] - o[c] if m == 3 else e[c] + o[c]
+                total[c] = total[c] + (both if m == 2 else 0.5 * both)
         for c in range(3):
             fr[c, pl.ds(t, SUB, stride=T), :] = total[c]
         return carry
 
-    steps(T, 2, to_rows, 0)
+    steps(T, UNROLL_SUM, to_rows, 0)
 
     def fold_group(group, carry):
         mask = (lane >= 8 * group) & (lane < 8 * group + 8)
@@ -518,24 +522,24 @@
     part = zero
     for n in range(2 * ITERS):
         part = jnp.where(sub == n, jnp.sum(mom[n], axis=0, keepdims=True), part)
-    ar1[me_x] = part
+    ar1[me_y] = part
+    col_sum = [
+        remote(ar1.at[me_y], ar1.at[me_y], sendr, recvr, o, peer(o, 0)) for o in range(1, ny)
+    ]
+    for x in col_sum:
+        x.start()
+    for x in col_sum:
+        x.wait_recv()
+    part = sum_all(ar1, ny)
+    ar2[me_x] = part
     row_sum = [
-        remote(ar1.at[me_x], ar1.at[me_x], sendr, recvr, o, peer(0, o)) for o in range(1, nx)
+        remote(ar2.at[me_x], ar2.at[me_x], sendc, recvc, o, peer(0, o)) for o in range(1, nx)
     ]
     for x in row_sum:
         x.start()
     for x in row_sum:
         x.wait_recv()
-    part = sum_all(ar1, nx)
-    ar2[me_y] = part
-    col_sum = [
-        remote(ar2.at[me_y], ar2.at[me_y], sendc, recvc, o, peer(o, 0)) for o in range(1, ny)
-    ]
-    for x in col_sum:
-        x.start()
-    for x in col_sum:
-        x.wait_recv()
-    whole = jnp.sum(sum_all(ar2, ny), axis=1, keepdims=True)
+    whole = jnp.sum(sum_all(ar2, nx), axis=1, keepdims=True)
     raw = [jnp.broadcast_to(whole[n : n + 1, :], (SUB, LANES)) for n in range(2 * ITERS)]
     nu = [raw[0], raw[1]]
     for n in range(2, 2 * ITERS):
@@ -596,8 +600,8 @@
         pltpu.VMEM((2, 32, LANES), f32),
         pltpu.VMEM((2, 32, LANES), f32),
         pltpu.VMEM((4,) + vreg, f32),
-        pltpu.VMEM((2 * REACH + 1, STEPS, 2) + vreg, f32),
-        pltpu.VMEM((2 * REACH + 1, STEPS + 1, 2) + vreg, jnp.int32),
+        pltpu.VMEM((km, STEPS, 2 * REACH, 2) + vreg, f32),
+        pltpu.VMEM((T + 1, 2 * REACH + 1, 2) + vreg, jnp.int32),
         pltpu.VMEM((3, ext + 2 * SUB, LANES), f32),
         pltpu.VMEM((3, ext + 2 * SUB, LANES), f32),
         pltpu.VMEM((2, 24, LANES), f32),
@@ -611,18 +615,18 @@
         pltpu.VMEM((T + 2, 3) + vreg, f32),
         pltpu.VMEM((ITERS + 2, T, 3) + vreg, f32),
         pltpu.VMEM((2 * ITERS + 1,) + vreg, f32),
+        pltpu.VMEM((ny,) + vreg, f32),
         pltpu.VMEM((nx,) + vreg, f32),
-        pltpu.VMEM((ny,) + vreg, f32),
         dma((4,)),
         dma((km, 2)),
         dma((8,)),
         dma((8,)),
         dma((8,)),
         dma((8,)),
+        dma((ny,)),
+        dma((ny,)),
         dma((nx,)),
         dma((nx,)),
-        dma((ny,)),
-        dma((ny,)),
     ]
     hbm = pl.BlockSpec(memory_space=pltpu.HBM)
     vmem = pl.BlockSpec(memory_space=pltpu.VMEM)

time: 38.2 us -> 34.1 us (0.89)
  Pallas kernels: 37.5 us -> 33.3 us
    pallas_call x1, Pallas kernels: 36.7 us -> 32.5 us  [shards(): pl.pallas_call(functools.partial(kernel, (ny, nx, km, rows)), out_shape=p...]
where the time goes in v3:
time: 34.1 us; the launch traced here: 34 us
  Pallas kernels  33.3 us (98%)
  between operations  0.64 us (2%)
    pallas_call x1, Pallas kernels, shards(): pl.pallas_call(functools.partial(kernel, (ny, nx, km, rows)), out_shape=p...  32.5 us
    pallas_call x1, Pallas kernels, shards(): pl.pallas_call(functools.partial(write_out, rows), out_shape=(shape, shap...  0.82 us

profile of v3, /device:TPU:1, one launch (start us, length us, event | category | flops | bytes accessed | tf_op | source)
XLA Modules:
  0.0 34.0 jit_solution(11817337923133248234)
XLA Ops:
  0.6 32.5 %shard_map.59.ores = f32[2,2,272,128]{3,2,1,0:T(8,128)S(1)} custom-call(f32[8]{0:T(128)} %th.1, f32[3,8,256,256]{3,2,1,0:T(8,128)} %fields.1, s32[256,256]{1,0:T(8,128)} %level_count.1, f32[256,256]{1,0:T(8,128)} %old_pressure.1), custom_call_target="tpu_custom_call" | custom-call | tf_op jit(solution)/shard_map/pallas_call | solution.py:633
  33.1 0.8 %shard_map.60 = (f32[256,256]{1,0:T(8,128)}, f32[256,256]{1,0:T(8,128)}) custom-call(f32[2,2,272,128]{3,2,1,0:T(8,128)S(1)} %shard_map.59.ores), custom_call_target="tpu_custom_call" | custom-call | tf_op jit(solution)/shard_map/pallas_call | solution.py:644

commit v4 on v3

--- a/solution.py
+++ b/solution.py
@@ -12,7 +12,7 @@
 ITERS = 4
 STEPS = 38
 UNROLL = 19
-UNROLL_SUM = 2
+UNROLL_SUM = 17
 REACH = 3
 MESH = pl.DeviceIdType.MESH
 
@@ -163,6 +163,15 @@
     sub = lax.broadcasted_iota(jnp.int32, (SUB, LANES), 0)
     zero = jnp.zeros((SUB, LANES), jnp.float32)
 
+    def peer(dy, dx):
+        return (lax.rem(me_y + dy + ny, ny), lax.rem(me_x + dx + nx, nx))
+
+    peers = [peer(dy, 0) for dy in range(1, ny)] + [peer(0, dx) for dx in range(1, nx)]
+    peers += [peer(dy, dx) for dy in (1, -1) for dx in (1, -1)]
+    barrier = pltpu.get_barrier_semaphore()
+    for x in peers:
+        pl.semaphore_signal(barrier, inc=1, device_id=x, device_id_type=MESH)
+
     loads = []
     for c in range(2):
         cols = pl.ds(c * LANES, LANES)
@@ -186,15 +195,6 @@
         for c in range(2):
             field_copy(k, c).start()
 
-    def peer(dy, dx):
-        return (lax.rem(me_y + dy + ny, ny), lax.rem(me_x + dx + nx, nx))
-
-    peers = [peer(dy, 0) for dy in range(1, ny)] + [peer(0, dx) for dx in range(1, nx)]
-    peers += [peer(dy, dx) for dy in (1, -1) for dx in (1, -1)]
-    barrier = pltpu.get_barrier_semaphore()
-    for x in peers:
-        pl.semaphore_signal(barrier, inc=1, device_id=x, device_id_type=MESH)
-
     def clear(k, carry):
         for f in range(3):
             for c in range(2):
@@ -218,6 +218,14 @@
         return carry
 
     steps(T, 2, clear_sum, 0)
+
+    def clear_terms(n, carry):
+        for m in range(2 * REACH):
+            for c in range(2):
+                terms[0, n, m, c] = zero
+        return carry
+
+    steps(STEPS, 2, clear_terms, 0)
 
     for x in loads:
         x.wait()
@@ -297,7 +305,7 @@
                 odd = u0[c] + ((a2 + a0[c]) - 4.0 * a1[c])
                 here = ((e2 + e0[c]) + (p4_ + p0[c])) - 4.0 * (e1[c] + p2[c]) + (v0[c] + v0[c])
                 for m, term in enumerate([u0[c], b - a1[c], d - odd, here, d + odd, b + a1[c]]):
-                    terms[k, n, m, c] = term
+                    terms[k + 1, n, m, c] = terms[k, n, m, c] + term
                 row = (u1[c], u2_, a1[c], a2, v1[c], v2, e1[c], e2, p1[c], p2[c], p3[c], p4_)
                 for x, y in zip(out, row):
                     x.append(y)
@@ -311,24 +319,24 @@
     for x in first:
         x.wait_recv()
 
-    def place(at, west_side, east_side, group):
-        lev_w = roll(west_side, 112 - 16 * group)
-        old_w = roll(west_side, 120 - 16 * group)
-        lev_e = roll(east_side, -16 * group)
-        old_e = roll(east_side, -16 * group - 8)
-        lp[0, 2, at, :] = jnp.where(lane < 64, lev_e, lev_w)
-        lp[1, 2, at, :] = jnp.where(lane < 64, old_e, old_w)
-
-    def unpack_group(group, carry):
-        for pos in range(4):
-            row = pl.ds(pos * SUB, SUB)
-            at = pl.ds(low + pl.multiple_of((pos * 8 + group) * SUB, SUB), SUB)
-            place(at, got1[0, row, :], got1[1, row, :], group)
-        return carry
-
-    steps(8, 2, unpack_group, 0)
-    place(pl.ds(PAD, SUB), got1d[0], got1d[1], 7)
-    place(pl.ds(high + SUB, SUB), got1d[2], got1d[3], 0)
+    def unpack(n, shift_west, shift_east):
+        def place(at, west_side, east_side, group):
+            west = roll(west_side, shift_west - 16 * group)
+            east = roll(east_side, shift_east - 16 * group)
+            lp[n, 2, at, :] = jnp.where(lane < 64, east, west)
+
+        def unpack_group(group, carry):
+            for pos in range(4):
+                row = pl.ds(pos * SUB, SUB)
+                at = pl.ds(low + pl.multiple_of((pos * 8 + group) * SUB, SUB), SUB)
+                place(at, got1[0, row, :], got1[1, row, :], group)
+            return carry
+
+        steps(8, 4, unpack_group, 0)
+        place(pl.ds(PAD, SUB), got1d[0], got1d[1], 7)
+        place(pl.ds(high + SUB, SUB), got1d[2], got1d[3], 0)
+
+    unpack(0, 112, 0)
 
     def shift_counts(group, carry):
         words = []
@@ -349,7 +357,7 @@
                     lcs[group * 7 + r, m + REACH, c] = (moved[c] >> (4 * r)) & 15
         return carry
 
-    steps(-(-T // 7), 1, shift_counts, 0)
+    steps(-(-T // 7), 5, shift_counts, 0)
 
     def to_rows(t, carry):
         tiles = []
@@ -357,10 +365,9 @@
             sums = []
             for c in range(2):
                 count = lcs[t, m, c]
-                total = None
+                total = 0.0
                 for k in range(km):
-                    term = jnp.where(count > k, terms[k, t + before, m % (2 * REACH), c], 0.0)
-                    total = term if k == 0 else total + term
+                    total = jnp.where(count > k, terms[k + 1, t + before, m % (2 * REACH), c], total)
                 sums.append(total)
             tiles.append(sums + [None])
         total = [tiles[REACH][0], tiles[REACH][1], 0.0]
@@ -387,7 +394,7 @@
             out.append(jnp.where(mask, west, carry[2 * pos + 1]))
         return tuple(out)
 
-    folded = steps(12, 2, fold_group, (zero,) * 6)
+    folded = steps(12, 6, fold_group, (zero,) * 6)
     for side in range(2):
         for pos in range(3):
             fold[side, pl.ds(pos * SUB, SUB), :] = folded[2 * pos + side]
@@ -403,6 +410,9 @@
     ]
     for x in second:
         x.start()
+    unpack(1, 120, -8)
+    for x in first:
+        x.wait_send()
 
     def depth_of(t):
         out = []
@@ -457,7 +467,7 @@
             ft[2, at, :] = fr[2, at, :] + jnp.where(lane < 4, west, jnp.where(lane >= 124, east, 0.0))
         return carry
 
-    steps(12, 2, gather_group, 0)
+    steps(12, 6, gather_group, 0)
     for n in range(2):
         for side in range(2):
             row = pl.ds(n * SUB, SUB)
@@ -482,7 +492,7 @@
                 out.append(carry[c] + (dm[t + 2, c] * z) * z)
         return tuple(out)
 
-    acc = steps(T, 2, residual_step, (zero, zero))
+    acc = steps(T, 17, residual_step, (zero, zero))
     mom[0] = acc[0] + acc[1]
 
     def power(k, carry):
@@ -528,6 +538,8 @@
     ]
     for x in col_sum:
         x.start()
+    for x in second:
+        x.wait_send()
     for x in col_sum:
         x.wait_recv()
     part = sum_all(ar1, ny)
@@ -537,6 +549,8 @@
     ]
     for x in row_sum:
         x.start()
+    for x in col_sum:
+        x.wait_send()
     for x in row_sum:
         x.wait_recv()
     whole = jnp.sum(sum_all(ar2, nx), axis=1, keepdims=True)
@@ -560,8 +574,8 @@
             ores[1, c, pl.ds(t, SUB, stride=T), :] = dm[t + 2, c] * value
         return carry
 
-    steps(T, 2, output_step, 0)
-    for x in first + second + row_sum + col_sum:
+    steps(T, 17, output_step, 0)
+    for x in row_sum:
         x.wait_send()
 
 
@@ -600,7 +614,7 @@
         pltpu.VMEM((2, 32, LANES), f32),
         pltpu.VMEM((2, 32, LANES), f32),
         pltpu.VMEM((4,) + vreg, f32),
-        pltpu.VMEM((km, STEPS, 2 * REACH, 2) + vreg, f32),
+        pltpu.VMEM((km + 1, STEPS, 2 * REACH, 2) + vreg, f32),
         pltpu.VMEM((T + 1, 2 * REACH + 1, 2) + vreg, jnp.int32),
         pltpu.VMEM((3, ext + 2 * SUB, LANES), f32),
         pltpu.VMEM((3, ext + 2 * SUB, LANES), f32),

time: 34.1 us -> 31.4 us (0.921)
  Pallas kernels: 33.3 us -> 30.7 us
    pallas_call x1, Pallas kernels: 32.5 us -> 29.9 us  [shards(): pl.pallas_call(functools.partial(kernel, (ny, nx, km, rows)), out_shape=p...]
where the time goes in v4:
time: 31.4 us; the launch traced here: 31.3 us
  Pallas kernels  30.7 us (98%)
  between operations  0.64 us (2%)
    pallas_call x1, Pallas kernels, shards(): pl.pallas_call(functools.partial(kernel, (ny, nx, km, rows)), out_shape=p...  29.9 us
    pallas_call x1, Pallas kernels, shards(): pl.pallas_call(functools.partial(write_out, rows), out_shape=(shape, shap...  0.82 us

profile of v4, /device:TPU:1, one launch (start us, length us, event | category | flops | bytes accessed | tf_op | source)
XLA Modules:
  0.0 31.3 jit_solution(11822987560750332022)
XLA Ops:
  0.6 29.9 %shard_map.59.ores = f32[2,2,272,128]{3,2,1,0:T(8,128)S(1)} custom-call(f32[8]{0:T(128)} %th.1, f32[3,8,256,256]{3,2,1,0:T(8,128)} %fields.1, s32[256,256]{1,0:T(8,128)} %level_count.1, f32[256,256]{1,0:T(8,128)} %old_pressure.1), custom_call_target="tpu_custom_call" | custom-call | tf_op jit(solution)/shard_map/pallas_call | solution.py:647
  30.5 0.8 %shard_map.60 = (f32[256,256]{1,0:T(8,128)}, f32[256,256]{1,0:T(8,128)}) custom-call(f32[2,2,272,128]{3,2,1,0:T(8,128)S(1)} %shard_map.59.ores), custom_call_target="tpu_custom_call" | custom-call | tf_op jit(solution)/shard_map/pallas_call | solution.py:658

commit v5 on v4

--- a/solution.py
+++ b/solution.py
@@ -195,38 +195,6 @@
         for c in range(2):
             field_copy(k, c).start()
 
-    def clear(k, carry):
-        for f in range(3):
-            for c in range(2):
-                for r in (0, 8, rows + 16, rows + 24):
-                    fb[f, k, c, pl.ds(r, SUB), :] = zero
-        return carry
-
-    lax.fori_loop(0, km, clear, 0)
-    for n in range(2):
-        for c in range(3):
-            lp[n, c, pl.ds(0, SUB), :] = zero
-            lp[n, c, pl.ds(ext + PAD, SUB), :] = zero
-
-    for c in range(3):
-        for r in range(T, T + 2):
-            fr[c, pl.ds(r * SUB, SUB), :] = zero
-
-    def clear_sum(t, carry):
-        for c in range(3):
-            tk[0, t, c] = zero
-        return carry
-
-    steps(T, 2, clear_sum, 0)
-
-    def clear_terms(n, carry):
-        for m in range(2 * REACH):
-            for c in range(2):
-                terms[0, n, m, c] = zero
-        return carry
-
-    steps(STEPS, 2, clear_terms, 0)
-
     for x in loads:
         x.wait()
 
@@ -245,7 +213,7 @@
             out.append(jnp.where(mask, roll(west, 16 * group), carry[2 * pos + 1]))
         return tuple(out)
 
-    packed = steps(8, 2, pack_group, (zero,) * 8)
+    packed = steps(8, 8, pack_group, (zero,) * 8)
     for side in range(2):
         for pos in range(4):
             pack[side, pl.ds(pos * SUB, SUB), :] = packed[2 * pos + side]
@@ -275,6 +243,39 @@
     ]
     for x in first:
         x.start()
+
+    def clear(k, carry):
+        for f in range(3):
+            for c in range(2):
+                for r in (0, 8, rows + 16, rows + 24):
+                    fb[f, k, c, pl.ds(r, SUB), :] = zero
+        return carry
+
+    lax.fori_loop(0, km, clear, 0)
+    for n in range(2):
+        for c in range(3):
+            lp[n, c, pl.ds(0, SUB), :] = zero
+            lp[n, c, pl.ds(ext + PAD, SUB), :] = zero
+
+    for c in range(3):
+        for r in range(T, T + 2):
+            fr[c, pl.ds(r * SUB, SUB), :] = zero
+
+    def clear_sum(t, carry):
+        for c in range(3):
+            tk[0, t, c] = zero
+        return carry
+
+    steps(T, 2, clear_sum, 0)
+
+    def clear_terms(n, carry):
+        for m in range(2 * REACH):
+            for c in range(2):
+                terms[0, n, m, c] = zero
+        return carry
+
+    steps(STEPS, 2, clear_terms, 0)
+
     def row_of(t):
         return pl.ds(t + PAD, SUB, stride=T)
 
@@ -332,7 +333,7 @@
                 place(at, got1[0, row, :], got1[1, row, :], group)
             return carry
 
-        steps(8, 4, unpack_group, 0)
+        steps(8, 8, unpack_group, 0)
         place(pl.ds(PAD, SUB), got1d[0], got1d[1], 7)
         place(pl.ds(high + SUB, SUB), got1d[2], got1d[3], 0)
 
@@ -394,7 +395,7 @@
             out.append(jnp.where(mask, west, carry[2 * pos + 1]))
         return tuple(out)
 
-    folded = steps(12, 6, fold_group, (zero,) * 6)
+    folded = steps(12, 12, fold_group, (zero,) * 6)
     for side in range(2):
         for pos in range(3):
             fold[side, pl.ds(pos * SUB, SUB), :] = folded[2 * pos + side]
@@ -467,7 +468,7 @@
             ft[2, at, :] = fr[2, at, :] + jnp.where(lane < 4, west, jnp.where(lane >= 124, east, 0.0))
         return carry
 
-    steps(12, 6, gather_group, 0)
+    steps(12, 12, gather_group, 0)
     for n in range(2):
         for side in range(2):
             row = pl.ds(n * SUB, SUB)
@@ -532,6 +533,9 @@
     part = zero
     for n in range(2 * ITERS):
         part = jnp.where(sub == n, jnp.sum(mom[n], axis=0, keepdims=True), part)
+    for by in (64, 32, 16):
+        part = part + roll(part, by)
+    part = jnp.sum(jnp.where(lane // 16 == sub, part, 0.0), axis=0, keepdims=True)
     ar1[me_y] = part
     col_sum = [
         remote(ar1.at[me_y], ar1.at[me_y], sendr, recvr, o, peer(o, 0)) for o in range(1, ny)
@@ -553,8 +557,10 @@
         x.wait_send()
     for x in row_sum:
         x.wait_recv()
-    whole = jnp.sum(sum_all(ar2, nx), axis=1, keepdims=True)
-    raw = [jnp.broadcast_to(whole[n : n + 1, :], (SUB, LANES)) for n in range(2 * ITERS)]
+    whole = sum_all(ar2, nx)
+    for by in (8, 4, 2, 1):
+        whole = whole + pltpu.roll(whole, LANES - by, axis=1)
+    raw = [jnp.broadcast_to(whole[:, 16 * n : 16 * n + 1], (SUB, LANES)) for n in range(2 * ITERS)]
     nu = [raw[0], raw[1]]
     for n in range(2, 2 * ITERS):
         nu.append(2.0 * raw[n] - nu[n % 2])
@@ -629,8 +635,8 @@
         pltpu.VMEM((T + 2, 3) + vreg, f32),
         pltpu.VMEM((ITERS + 2, T, 3) + vreg, f32),
         pltpu.VMEM((2 * ITERS + 1,) + vreg, f32),
-        pltpu.VMEM((ny,) + vreg, f32),
-        pltpu.VMEM((nx,) + vreg, f32),
+        pltpu.VMEM((ny, 1, LANES), f32),
+        pltpu.VMEM((nx, 1, LANES), f32),
         dma((4,)),
         dma((km, 2)),
         dma((8,)),

time: 31.4 us -> 31.2 us (level)
  Pallas kernels: 30.7 us -> 30.3 us
    pallas_call x1, Pallas kernels: 29.9 us -> 29.5 us  [shards(): pl.pallas_call(functools.partial(kernel, (ny, nx, km, rows)), out_shape=p...]
where the time goes in v5:
time: 31.2 us; the launch traced here: 30.9 us
  Pallas kernels  30.3 us (97%)
  between operations  0.64 us (2%)
    pallas_call x1, Pallas kernels, shards(): pl.pallas_call(functools.partial(kernel, (ny, nx, km, rows)), out_shape=p...  29.5 us
    pallas_call x1, Pallas kernels, shards(): pl.pallas_call(functools.partial(write_out, rows), out_shape=(shape, shap...  0.82 us

profile of v5, /device:TPU:1, one launch (start us, length us, event | category | flops | bytes accessed | tf_op | source)
XLA Modules:
  0.0 30.9 jit_solution(10655344380131635392)
XLA Ops:
  0.6 29.5 %shard_map.59.ores = f32[2,2,272,128]{3,2,1,0:T(8,128)S(1)} custom-call(f32[8]{0:T(128)} %th.1, f32[3,8,256,256]{3,2,1,0:T(8,128)} %fields.1, s32[256,256]{1,0:T(8,128)} %level_count.1, f32[256,256]{1,0:T(8,128)} %old_pressure.1), custom_call_target="tpu_custom_call" | custom-call | tf_op jit(solution)/shard_map/pallas_call | solution.py:653
  30.1 0.8 %shard_map.60 = (f32[256,256]{1,0:T(8,128)}, f32[256,256]{1,0:T(8,128)}) custom-call(f32[2,2,272,128]{3,2,1,0:T(8,128)S(1)} %shard_map.59.ores), custom_call_target="tpu_custom_call" | custom-call | tf_op jit(solution)/shard_map/pallas_call | solution.py:664

commit v6 on v5

--- a/solution.py
+++ b/solution.py
@@ -12,7 +12,7 @@
 ITERS = 4
 STEPS = 38
 UNROLL = 19
-UNROLL_SUM = 17
+UNROLL_SUM = 34
 REACH = 3
 MESH = pl.DeviceIdType.MESH
 
@@ -452,7 +452,7 @@
                 dm[n, c] = jnp.where(outside, 0.0, diagonal)
         return depth1, mid1, west1, down1, down2, k1, guess1
 
-    steps(T + 2, 4, coefficient_step, (depth_of(-1),) + ([zero] * 3,) * 6)
+    steps(T + 2, 12, coefficient_step, (depth_of(-1),) + ([zero] * 3,) * 6)
 
     for x in second:
         x.wait_recv()

time: 31.2 us -> 31.1 us (level)
  no operation moved by 1% of the time
where the time goes in v6:
time: 31.1 us; the launch traced here: 30.8 us
  Pallas kernels  30.2 us (97%)
  between operations  0.64 us (2%)
    pallas_call x1, Pallas kernels, shards(): pl.pallas_call(functools.partial(kernel, (ny, nx, km, rows)), out_shape=p...  29.4 us
    pallas_call x1, Pallas kernels, shards(): pl.pallas_call(functools.partial(write_out, rows), out_shape=(shape, shap...  0.82 us

profile of v6, /device:TPU:1, one launch (start us, length us, event | category | flops | bytes accessed | tf_op | source)
XLA Modules:
  0.0 30.8 jit_solution(17709962635366479716)
XLA Ops:
  0.6 29.4 %shard_map.59.ores = f32[2,2,272,128]{3,2,1,0:T(8,128)S(1)} custom-call(f32[8]{0:T(128)} %th.1, f32[3,8,256,256]{3,2,1,0:T(8,128)} %fields.1, s32[256,256]{1,0:T(8,128)} %level_count.1, f32[256,256]{1,0:T(8,128)} %old_pressure.1), custom_call_target="tpu_custom_call" | custom-call | tf_op jit(solution)/shard_map/pallas_call | solution.py:653
  30.0 0.8 %shard_map.60 = (f32[256,256]{1,0:T(8,128)}, f32[256,256]{1,0:T(8,128)}) custom-call(f32[2,2,272,128]{3,2,1,0:T(8,128)S(1)} %shard_map.59.ores), custom_call_target="tpu_custom_call" | custom-call | tf_op jit(solution)/shard_map/pallas_call | solution.py:664
